TPU v7x, 128 devices: a whole 4x4x4 slice. The times are simulated.
128 devices in a mesh: cx: 16 (over y_lo, x, core), cy: 8 (over y_hi, z).
Axes of the slice: x: 4, y: 4 (y_hi: 2, y_lo: 2; y = y_hi * 2 + y_lo), z: 4, core: 2. Of those that a mesh axis runs over, the one named last changes fastest.
Arguments:
- signal: float32 [16384, 1024], P(('cx', 'cy')), may hold values from -6 to 6
- fan_cut: int32 [16384], replicated, may hold values from 0 to 255
Outputs:
- correlation: float32 [16384, 4096], P(('cx', 'cy'))
All inputs are finite; a program needn't handle non-finite values.
Results may differ from a plain program's by a relative error of at most 0.0032.
Values may be sent and summed in bfloat16 or wider, within the bound.
A program may use at most 64 MiB of HBM per device.

v0:
```python
import functools
import math

import jax
import jax.numpy as jnp
import numpy as np
from jax import lax
from jax.experimental import pallas as pl
from jax.experimental.pallas import tpu as pltpu
from jax.sharding import PartitionSpec as P

BAND = 256
LAGS = 16
BINS = 256
OWN = 128
LENGTH = 1024
MESH = pl.DeviceIdType.MESH
F32 = jnp.float32
BF16 = jnp.bfloat16


def halves(table):
    high = table.astype(BF16)
    return high, (table - high.astype(np.float64)).astype(BF16)


def tables(groups):
    bin_index = np.arange(BINS, dtype=np.int64)
    angle = 2.0 * math.pi / LENGTH * (bin_index[:, None] * np.arange(LENGTH)[None, :] % LENGTH)
    pairs = np.stack([np.cos(angle), -np.sin(angle)], axis=1).reshape(groups, 2, 2, LENGTH)
    time = pairs.transpose(0, 2, 1, 3).reshape(2 * BINS, LENGTH)
    index = np.arange(groups)
    angle = 2.0 * math.pi / groups * (index[:, None] * index[None, :] % groups)
    re, im = np.cos(angle), -np.sin(angle)
    wide = np.block([[re, -im], [im, re]])
    angle = 2.0 * math.pi / (groups * OWN) * (index[:, None] * index[None, :])
    twist = np.stack([np.cos(angle), np.sin(angle)]).astype(np.float32)
    return (*halves(time), *halves(wide), *halves(wide.T), twist)


def dot(left, right, dims=((1,), (0,))):
    return lax.dot_general(left, right, (dims, ((), ())), preferred_element_type=F32)


def split(value):
    high = value.astype(BF16)
    return high, (value - high.astype(F32)).astype(BF16)


def dot_three(left, right):
    return dot(left[0], right[0]) + (dot(left[0], right[1]) + dot(left[1], right[0]))


def blocks(value):
    return value[:OWN, :OWN], value[:OWN, OWN:], value[OWN:, :OWN], value[OWN:, OWN:]


def join(a, b, c, d):
    return jnp.concatenate([jnp.concatenate([a, b], axis=1), jnp.concatenate([c, d], axis=1)], axis=0)


def least_cut(cut):
    row = lax.broadcasted_iota(jnp.int32, (OWN, OWN), 0)
    col = lax.broadcasted_iota(jnp.int32, (OWN, OWN), 1)
    mirror = (((row + col) % OWN) == 0).astype(F32).astype(BF16)
    reverse = ((row + col) == OWN - 1).astype(F32).astype(BF16)
    exact = cut.astype(F32).astype(BF16)
    across = dot(exact, mirror).astype(BF16)
    mirrored = jnp.where(col == 0, dot(mirror, across), dot(reverse, across))
    return jnp.maximum(cut.astype(F32), mirrored).T


def filter_kernel(
    groups, inner,
    signal, cut, time_high, time_low, wide_high, wide_low, flip_high, flip_low, twist,
    ext,
    out_first, in_first, out_second, in_second,
    send_first, recv_first, send_second, recv_second, send_halo, recv_halo,
):
    me = lax.axis_index("cx") * inner + lax.axis_index("cy")

    def at(device):
        return (device // inner, device % inner)

    def peer(step):
        return lax.rem(me + step, groups)

    barrier = pltpu.get_barrier_semaphore()

    def greet(step, carry):
        pl.semaphore_signal(barrier, inc=1, device_id=at(peer(step)), device_id_type=MESH)
        return carry

    lax.fori_loop(1, groups, greet, 0)

    own_high, own_low = split(signal[...])
    both = jnp.concatenate([own_high, own_low], axis=0)
    wide_sum = dot(time_high[...], both, ((1,), (1,)))
    spectrum = (wide_sum[:, :OWN] + wide_sum[:, OWN:]) + dot(time_low[...], own_high, ((1,), (1,)))
    out_first[...] = spectrum.reshape(groups, 4, OWN)

    pl.semaphore_wait(barrier, groups - 1)

    def exchange(outgoing, incoming, send_sem, recv_sem):
        def push(step, carry):
            target = peer(step)
            pltpu.make_async_remote_copy(
                src_ref=outgoing.at[target],
                dst_ref=incoming.at[me],
                send_sem=send_sem,
                recv_sem=recv_sem,
                device_id=at(target),
                device_id_type=MESH,
            ).start()
            return carry

        lax.fori_loop(1, groups, push, 0)
        incoming[me] = outgoing[me]

    def settle(outgoing, incoming, send_sem, recv_sem):
        rest = pltpu.make_async_remote_copy(
            src_ref=outgoing.at[pl.ds(0, groups - 1)],
            dst_ref=incoming.at[pl.ds(0, groups - 1)],
            send_sem=send_sem,
            recv_sem=recv_sem,
            device_id=at(peer(1)),
            device_id_type=MESH,
        )
        rest.wait()

    exchange(out_first, in_first, send_first, recv_first)
    cut_least = least_cut(cut[...])
    wide = (wide_high[...], wide_low[...])
    flip = (flip_high[...], flip_low[...])
    cosine, sine = twist[0], twist[1]
    settle(out_first, in_first, send_first, recv_first)

    rows = [in_first[:, part, :] for part in range(4)]
    value = dot_three(wide, split(join(*rows)))
    re_a, re_b, im_a, im_b = blocks(value)
    value = join(
        re_a * cosine + im_a * sine, im_a * cosine - re_a * sine,
        re_b * cosine + im_b * sine, im_b * cosine - re_b * sine,
    )
    value = dot_three(split(value), flip)
    even = (2 * me).astype(F32)
    scale = -2.0 / (LENGTH * groups * OWN)
    keep_a = jnp.where(cut_least > even, jnp.where(me == 0, 0.5 * scale, scale), 0.0)
    keep_b = jnp.where(cut_least > even + 1.0, scale, 0.0)
    value = value * join(keep_a, keep_a, keep_b, keep_b)
    value = dot_three(split(value), wide)
    re_a, im_a, re_b, im_b = blocks(value)
    value = join(
        re_a * cosine - im_a * sine, re_b * cosine - im_b * sine,
        im_a * cosine + re_a * sine, im_b * cosine + re_b * sine,
    )
    value = dot_three(flip, split(value))
    for part, block in enumerate(blocks(value)):
        out_second[:, part, :] = block

    exchange(out_second, in_second, send_second, recv_second)
    settle(out_second, in_second, send_second, recv_second)

    back_high, back_low = split(in_second[...].reshape(4 * groups, OWN).T)
    both = jnp.concatenate([back_high, back_low], axis=0)
    halos = []
    chunk = 256
    for number in range(LENGTH // chunk):
        span = pl.ds(number * chunk, chunk)
        high, low = time_high[:, span], time_low[:, span]
        sums = dot(both, high)
        rejected = (sums[:OWN] + sums[OWN:]) + dot(back_high, low)
        ext[pl.ds(OWN, OWN), span] = (signal[:, span] + rejected).astype(BF16)
        source = ext.at[pl.ds(OWN, OWN), span]
        halos.append((
            pltpu.make_async_remote_copy(
                src_ref=source, dst_ref=ext.at[pl.ds(0, OWN), span],
                send_sem=send_halo.at[0, number], recv_sem=recv_halo.at[0, number],
                device_id=at(peer(1)), device_id_type=MESH,
            ),
            pltpu.make_async_remote_copy(
                src_ref=source, dst_ref=ext.at[pl.ds(2 * OWN, OWN), span],
                send_sem=send_halo.at[1, number], recv_sem=recv_halo.at[1, number],
                device_id=at(peer(groups - 1)), device_id_type=MESH,
            ),
        ))
        for copy in halos[-1]:
            copy.start()
    for pair in halos:
        for copy in pair:
            copy.wait()

    @pl.when(me == 0)
    def _():
        ext[pl.ds(0, OWN), :] = jnp.zeros((OWN, LENGTH), BF16)

    @pl.when(me == groups - 1)
    def _():
        ext[pl.ds(2 * OWN, OWN), :] = jnp.zeros((OWN, LENGTH), BF16)


def correlate_kernel(ext, out, lagged):
    own = ext[pl.ds(OWN, OWN), :] * jnp.asarray(1.0 / math.sqrt(LENGTH), BF16)

    def shifted(lag):
        if lag == 0:
            return own
        return jnp.concatenate([jnp.zeros((OWN, lag), BF16), own[:, :LENGTH - lag]], axis=1)

    everything = ext[...]
    count = ext.shape[0]
    for lag in range(0, LAGS, 2):
        pair = jnp.concatenate([shifted(lag), shifted(lag + 1)], axis=0)
        products = dot(everything, pair, ((1,), (1,)))
        lagged[pl.ds(lag, count, stride=LAGS), :] = products[:, :OWN]
        lagged[pl.ds(lag + 1, count, stride=LAGS), :] = products[:, OWN:]
    lane = lax.broadcasted_iota(jnp.int32, (8, OWN), 1)
    odd = [(lane // step) % 2 == 1 for step in (1, 2, 4)]
    tiles = BAND * LAGS // OWN
    for tile in range(tiles + OWN // 8 - 1):
        rows = [lagged[pl.ds(tile * OWN + 8 * number, 8), :] for number in range(OWN // 8 + 14)]
        for bit in range(3):
            gap = 2 << bit
            rows = [jnp.where(odd[bit], rows[at + gap], rows[at]) for at in range(len(rows) - gap)]
        turned = jnp.concatenate(rows, axis=0).T
        for group in range(max(0, tile - tiles + 1), min(OWN // 8, tile + 1)):
            out[pl.ds(8 * group, 8), (tile - group) * OWN:(tile - group + 1) * OWN] = turned[8 * group:8 * group + 8]


def body(groups, inner, signal, fan_cut):
    whole = pl.BlockSpec(memory_space=pltpu.VMEM)
    arrays = [jnp.asarray(table) for table in tables(groups)]
    message = pltpu.VMEM((groups, 4, OWN), F32)
    ext = pl.pallas_call(
        functools.partial(filter_kernel, groups, inner),
        out_shape=jax.ShapeDtypeStruct((3 * OWN, LENGTH), BF16),
        in_specs=[whole] * (2 + len(arrays)),
        out_specs=whole,
        scratch_shapes=[message] * 4 + [pltpu.SemaphoreType.DMA] * 4 + [pltpu.SemaphoreType.DMA((2, 4))] * 2,
        compiler_params=pltpu.CompilerParams(
            collective_id=0, has_side_effects=True, vmem_limit_bytes=40 * 2**20
        ),
        name="fan_filter",
    )(signal, fan_cut.reshape(OWN, groups), *arrays)
    return pl.pallas_call(
        correlate_kernel,
        out_shape=jax.ShapeDtypeStruct((OWN, BAND * LAGS), F32),
        in_specs=[whole],
        out_specs=whole,
        scratch_shapes=[pltpu.VMEM((3 * OWN * LAGS, OWN), F32)],
        compiler_params=pltpu.CompilerParams(vmem_limit_bytes=40 * 2**20),
        name="correlate",
    )(ext)


def solution(mesh):
    groups, inner = mesh.size, mesh.shape["cy"]
    return jax.shard_map(
        functools.partial(body, groups, inner),
        mesh=mesh,
        in_specs=(P(("cx", "cy"), None), P()),
        out_specs=P(("cx", "cy"), None),
        check_vma=False,
    )
```

profile of v0, /device:TPU:1, one launch (start us, length us, event | category | flops | bytes accessed | tf_op | source)
XLA Modules:
  0.0 51.5 jit_solution(15714724173622741863)
XLA Ops:
  0.0 0.0 copy-start
  0.0 1.2 %copy-done = bf16[512,1024]{1,0:T(8,128)(2,1)S(1)} copy-done((bf16[512,1024]{1,0:T(8,128)(2,1)S(1)}, bf16[512,1024]{1,0:T(8,128)(2,1)}, u32[]{:S(2)}) %copy-start) | copy-done | bytes 1048600
  1.2 0.0 copy-start.1
  1.2 1.2 %copy-done.1 = bf16[512,1024]{1,0:T(8,128)(2,1)S(1)} copy-done((bf16[512,1024]{1,0:T(8,128)(2,1)S(1)}, bf16[512,1024]{1,0:T(8,128)(2,1)}, u32[]{:S(2)}) %copy-start.1) | copy-done | bytes 1048600
  2.5 0.0 copy-start.2
  2.5 1.0 %copy-done.2 = f32[128,1024]{1,0:T(8,128)S(1)} copy-done((f32[128,1024]{1,0:T(8,128)S(1)}, f32[128,1024]{1,0:T(8,128)}, u32[]{:S(2)}) %copy-start.2) | copy-done | bytes 524312
  3.5 0.0 copy-start.3
  3.5 0.9 %copy-done.3 = f32[2,128,128]{2,1,0:T(8,128)S(1)} copy-done((f32[2,128,128]{2,1,0:T(8,128)S(1)}, f32[2,128,128]{2,1,0:T(8,128)}, u32[]{:S(2)}) %copy-start.3) | copy-done | bytes 131096
  4.4 0.0 copy-start.4
  4.4 0.9 %copy-done.4 = bf16[256,256]{1,0:T(8,128)(2,1)S(1)} copy-done((bf16[256,256]{1,0:T(8,128)(2,1)S(1)}, bf16[256,256]{1,0:T(8,128)(2,1)}, u32[]{:S(2)}) %copy-start.4) | copy-done | bytes 131096
  5.3 0.0 copy-start.5
  5.3 0.9 %copy-done.5 = bf16[256,256]{1,0:T(8,128)(2,1)S(1)} copy-done((bf16[256,256]{1,0:T(8,128)(2,1)S(1)}, bf16[256,256]{1,0:T(8,128)(2,1)}, u32[]{:S(2)}) %copy-start.5) | copy-done | bytes 131096
  6.2 0.0 copy-start.6
  6.2 0.9 %copy-done.6 = bf16[256,256]{1,0:T(8,128)(2,1)S(1)} copy-done((bf16[256,256]{1,0:T(8,128)(2,1)S(1)}, bf16[256,256]{1,0:T(8,128)(2,1)}, u32[]{:S(2)}) %copy-start.6) | copy-done | bytes 131096
  7.1 0.0 copy-start.7
  7.1 0.9 %copy-done.7 = bf16[256,256]{1,0:T(8,128)(2,1)S(1)} copy-done((bf16[256,256]{1,0:T(8,128)(2,1)S(1)}, bf16[256,256]{1,0:T(8,128)(2,1)}, u32[]{:S(2)}) %copy-start.7) | copy-done | bytes 131096
  8.0 0.0 copy-start.8
  8.0 0.8 %copy-done.8 = s32[16384]{0:T(1024)S(1)} copy-done((s32[16384]{0:T(1024)S(1)}, s32[16384]{0:T(1024)}, u32[]{:S(2)}) %copy-start.8) | copy-done | bytes 65560
  8.9 38.1 %fan_filter.1.ext = bf16[384,1024]{1,0:T(8,128)(2,1)S(1)} custom-call(f32[128,1024]{1,0:T(8,128)S(1)} %copy-done.2, s32[128,128]{1,0:T(8,128)S(1)} %bitcast.1, bf16[512,1024]{1,0:T(8,128)(2,1)S(1)} %copy-done.1, bf16[512,1024]{1,0:T(8,128)(2,1)S(1)} %copy-done, bf16[256,256]{1,0:T(8,128)(2,1)S(1)} %copy-done.7, bf16[256,256]{1,0:T(8,128)(2,1)S(1)} %copy-done.6, ...), custom_call_target="tpu_custom_call" | custom-call | tf_op jit(solution)/shard_map/fan_filter/pallas_call | solution.py:234
  46.9 4.6 %correlate.1 = f32[128,4096]{1,0:T(8,128)} custom-call(bf16[384,1024]{1,0:T(8,128)(2,1)S(1)} %fan_filter.1.ext), custom_call_target="tpu_custom_call" | custom-call | tf_op jit(solution)/shard_map/correlate/pallas_call | solution.py:245
Async XLA Ops:
  0.0 1.2 %copy-start = (bf16[512,1024]{1,0:T(8,128)(2,1)S(1)}, bf16[512,1024]{1,0:T(8,128)(2,1)}, u32[]{:S(2)}) copy-start(bf16[512,1024]{1,0:T(8,128)(2,1)} %constant.15.clone.time_low) | copy-start | bytes 3145732
  1.2 1.2 %copy-start.1 = (bf16[512,1024]{1,0:T(8,128)(2,1)S(1)}, bf16[512,1024]{1,0:T(8,128)(2,1)}, u32[]{:S(2)}) copy-start(bf16[512,1024]{1,0:T(8,128)(2,1)} %constant.14.clone.time_high) | copy-start | bytes 3145732
  2.5 1.0 %copy-start.2 = (f32[128,1024]{1,0:T(8,128)S(1)}, f32[128,1024]{1,0:T(8,128)}, u32[]{:S(2)}) copy-start(f32[128,1024]{1,0:T(8,128)} %signal.1) | copy-start | bytes 1572868
  3.5 0.9 %copy-start.3 = (f32[2,128,128]{2,1,0:T(8,128)S(1)}, f32[2,128,128]{2,1,0:T(8,128)}, u32[]{:S(2)}) copy-start(f32[2,128,128]{2,1,0:T(8,128)} %constant.20.clone.twist) | copy-start | bytes 393220
  4.4 0.9 %copy-start.4 = (bf16[256,256]{1,0:T(8,128)(2,1)S(1)}, bf16[256,256]{1,0:T(8,128)(2,1)}, u32[]{:S(2)}) copy-start(bf16[256,256]{1,0:T(8,128)(2,1)} %constant.19.clone.flip_low) | copy-start | bytes 393220
  5.3 0.9 %copy-start.5 = (bf16[256,256]{1,0:T(8,128)(2,1)S(1)}, bf16[256,256]{1,0:T(8,128)(2,1)}, u32[]{:S(2)}) copy-start(bf16[256,256]{1,0:T(8,128)(2,1)} %constant.18.clone.flip_high) | copy-start | bytes 393220
  6.2 0.9 %copy-start.6 = (bf16[256,256]{1,0:T(8,128)(2,1)S(1)}, bf16[256,256]{1,0:T(8,128)(2,1)}, u32[]{:S(2)}) copy-start(bf16[256,256]{1,0:T(8,128)(2,1)} %constant.17.clone.wide_low) | copy-start | bytes 393220
  7.1 0.9 %copy-start.7 = (bf16[256,256]{1,0:T(8,128)(2,1)S(1)}, bf16[256,256]{1,0:T(8,128)(2,1)}, u32[]{:S(2)}) copy-start(bf16[256,256]{1,0:T(8,128)(2,1)} %constant.16.clone.wide_high) | copy-start | bytes 393220
  8.0 0.8 %copy-start.8 = (s32[16384]{0:T(1024)S(1)}, s32[16384]{0:T(1024)}, u32[]{:S(2)}) copy-start(s32[16384]{0:T(1024)} %param.10) | copy-start | bytes 196612
where the time goes:
time: 51.9 us; the launch traced here: 51.5 us
  Pallas kernels  42.6 us (82%)
  local copies, waits for them, and re-layouts  8.85 us (17%)
    pallas_call x1, Pallas kernels, body(): pl.pallas_call(functools.partial(filter_kernel, groups, inner), out_shape...  38.1 us
    unnamed x18, local copies, waits for them, and re-layouts  8.85 us
    pallas_call x1, Pallas kernels, body(): pl.pallas_call(correlate_kernel, out_shape=jax.ShapeDtypeStruct((OWN, BAN...  4.59 us

commit v1 on v0

--- a/solution.py
+++ b/solution.py
@@ -35,7 +35,7 @@
     wide = np.block([[re, -im], [im, re]])
     angle = 2.0 * math.pi / (groups * OWN) * (index[:, None] * index[None, :])
     twist = np.stack([np.cos(angle), np.sin(angle)]).astype(np.float32)
-    return (*halves(time), *halves(wide), *halves(wide.T), twist)
+    return np.stack(halves(time)), np.stack([*halves(wide), *halves(wide.T)]), twist
 
 
 def dot(left, right, dims=((1,), (0,))):
@@ -72,12 +72,15 @@
 
 def filter_kernel(
     groups, inner,
-    signal, cut, time_high, time_low, wide_high, wide_low, flip_high, flip_low, twist,
-    ext,
+    signal_far, cut_far, time_far, wide_far, twist_far,
+    out_far,
+    signal, cut, time, wide_all, twist, load_sems,
     out_first, in_first, out_second, in_second,
     send_first, recv_first, send_second, recv_second, send_halo, recv_halo,
+    ext, lags, partial, lagged, out, store_sem,
 ):
-    me = lax.axis_index("cx") * inner + lax.axis_index("cy")
+    outer_at, inner_at = lax.axis_index("cx"), lax.axis_index("cy")
+    me = outer_at * inner + inner_at
 
     def at(device):
         return (device // inner, device % inner)
@@ -85,36 +88,64 @@
     def peer(step):
         return lax.rem(me + step, groups)
 
+    def visit_others(visit):
+        high, mid, core = outer_at // 8, lax.rem(outer_at // 2, 4), lax.rem(outer_at, 2)
+        top, low = inner_at // 4, lax.rem(inner_at, 4)
+        highs, cores, tops = [8 * high, 8 - 8 * high], [core, 1 - core], [4 * top, 4 - 4 * top]
+
+        def near(mid_step, low_step, combinations):
+            mid_to, low_to = 2 * lax.rem(mid + mid_step, 4), lax.rem(low + low_step, 4)
+            for flip_top, flip_high, flip_core in combinations:
+                visit(highs[flip_high] + mid_to + cores[flip_core], tops[flip_top] + low_to)
+
+        every = [(i, j, k) for i in (1, 0) for j in (1, 0) for k in (1, 0)]
+
+        def far(number):
+            return number + 2 - (number // 2) * (2 * number - 1)
+
+        def block(index, carry):
+            near(far(index // 4), far(lax.rem(index, 4)), every)
+            return carry
+
+        lax.fori_loop(0, 15, block, 0)
+        near(0, 0, every[:-1])
+
+    pairs = ((signal_far, signal), (time_far.at[0], time.at[0]), (time_far.at[1], time.at[1]),
+             (cut_far, cut), (wide_far, wide_all), (twist_far, twist))
+    loads = [pltpu.make_async_copy(far, near, load_sems.at[number]) for number, (far, near) in enumerate(pairs)]
+    for load in loads:
+        load.start()
+
     barrier = pltpu.get_barrier_semaphore()
 
-    def greet(step, carry):
-        pl.semaphore_signal(barrier, inc=1, device_id=at(peer(step)), device_id_type=MESH)
-        return carry
-
-    lax.fori_loop(1, groups, greet, 0)
-
+    def greet(cx, cy):
+        pl.semaphore_signal(barrier, inc=1, device_id=(cx, cy), device_id_type=MESH)
+
+    visit_others(greet)
+    loads[0].wait()
+    time_high, time_low = time.at[0], time.at[1]
     own_high, own_low = split(signal[...])
     both = jnp.concatenate([own_high, own_low], axis=0)
+    loads[1].wait()
     wide_sum = dot(time_high[...], both, ((1,), (1,)))
+    loads[2].wait()
     spectrum = (wide_sum[:, :OWN] + wide_sum[:, OWN:]) + dot(time_low[...], own_high, ((1,), (1,)))
     out_first[...] = spectrum.reshape(groups, 4, OWN)
 
     pl.semaphore_wait(barrier, groups - 1)
 
     def exchange(outgoing, incoming, send_sem, recv_sem):
-        def push(step, carry):
-            target = peer(step)
+        def push(cx, cy):
             pltpu.make_async_remote_copy(
-                src_ref=outgoing.at[target],
+                src_ref=outgoing.at[cx * inner + cy],
                 dst_ref=incoming.at[me],
                 send_sem=send_sem,
                 recv_sem=recv_sem,
-                device_id=at(target),
+                device_id=(cx, cy),
                 device_id_type=MESH,
             ).start()
-            return carry
-
-        lax.fori_loop(1, groups, push, 0)
+
+        visit_others(push)
         incoming[me] = outgoing[me]
 
     def settle(outgoing, incoming, send_sem, recv_sem):
@@ -129,9 +160,11 @@
         rest.wait()
 
     exchange(out_first, in_first, send_first, recv_first)
+    for load in loads[3:]:
+        load.wait()
     cut_least = least_cut(cut[...])
-    wide = (wide_high[...], wide_low[...])
-    flip = (flip_high[...], flip_low[...])
+    wide = (wide_all[0], wide_all[1])
+    flip = (wide_all[2], wide_all[3])
     cosine, sine = twist[0], twist[1]
     settle(out_first, in_first, send_first, recv_first)
 
@@ -186,71 +219,104 @@
         ))
         for copy in halos[-1]:
             copy.start()
-    for pair in halos:
-        for copy in pair:
-            copy.wait()
-
-    @pl.when(me == 0)
-    def _():
-        ext[pl.ds(0, OWN), :] = jnp.zeros((OWN, LENGTH), BF16)
-
-    @pl.when(me == groups - 1)
-    def _():
-        ext[pl.ds(2 * OWN, OWN), :] = jnp.zeros((OWN, LENGTH), BF16)
-
-
-def correlate_kernel(ext, out, lagged):
     own = ext[pl.ds(OWN, OWN), :] * jnp.asarray(1.0 / math.sqrt(LENGTH), BF16)
-
-    def shifted(lag):
-        if lag == 0:
-            return own
-        return jnp.concatenate([jnp.zeros((OWN, lag), BF16), own[:, :LENGTH - lag]], axis=1)
-
-    everything = ext[...]
-    count = ext.shape[0]
-    for lag in range(0, LAGS, 2):
-        pair = jnp.concatenate([shifted(lag), shifted(lag + 1)], axis=0)
-        products = dot(everything, pair, ((1,), (1,)))
-        lagged[pl.ds(lag, count, stride=LAGS), :] = products[:, :OWN]
-        lagged[pl.ds(lag + 1, count, stride=LAGS), :] = products[:, OWN:]
+    for lag in range(LAGS):
+        lags[pl.ds(lag * OWN, OWN), :] = own if lag == 0 else jnp.concatenate(
+            [jnp.zeros((OWN, lag), BF16), own[:, :LENGTH - lag]], axis=1
+        )
+
+    def products(rows, number, begin, length):
+        return dot(rows, lags[pl.ds(number * 2 * OWN, 2 * OWN), begin:begin + length], ((1,), (1,)))
+
+    def keep(block, number, values):
+        for side in range(2):
+            begin = block * OWN * LAGS + 2 * number + side
+            lagged[pl.ds(begin, OWN, stride=LAGS), :] = values[:, side * OWN:(side + 1) * OWN]
+
     lane = lax.broadcasted_iota(jnp.int32, (8, OWN), 1)
     odd = [(lane // step) % 2 == 1 for step in (1, 2, 4)]
     tiles = BAND * LAGS // OWN
-    for tile in range(tiles + OWN // 8 - 1):
-        rows = [lagged[pl.ds(tile * OWN + 8 * number, 8), :] for number in range(OWN // 8 + 14)]
-        for bit in range(3):
-            gap = 2 << bit
-            rows = [jnp.where(odd[bit], rows[at + gap], rows[at]) for at in range(len(rows) - gap)]
-        turned = jnp.concatenate(rows, axis=0).T
-        for group in range(max(0, tile - tiles + 1), min(OWN // 8, tile + 1)):
-            out[pl.ds(8 * group, 8), (tile - group) * OWN:(tile - group + 1) * OWN] = turned[8 * group:8 * group + 8]
+    tile_rows = OWN // 8
+
+    def finish(first, last):
+        for tile in range(first, last):
+            rows = [lagged[pl.ds(tile * OWN + 8 * number, 8), :] for number in range(tile_rows + 14)]
+            for bit in range(3):
+                gap = 2 << bit
+                rows = [jnp.where(odd[bit], rows[spot + gap], rows[spot]) for spot in range(len(rows) - gap)]
+            turned = jnp.concatenate(rows, axis=0).T
+            for group in range(max(0, tile - tiles + 1), min(tile_rows, tile + 1)):
+                out[pl.ds(8 * group, 8), pl.ds((tile - group) * OWN, OWN)] = turned[8 * group:8 * group + 8]
+        for group in range(tile_rows):
+            begin, end = max(0, first - group), min(tiles, last - group)
+            if begin < end:
+                place = (pl.ds(8 * group, 8), pl.ds(begin * OWN, (end - begin) * OWN))
+                pltpu.make_async_copy(out.at[place], out_far.at[place], store_sem).start()
+
+    middle = ext[pl.ds(OWN, OWN), :]
+    for number in range(LAGS // 2):
+        keep(1, number, products(middle, number, 0, LENGTH))
+    finish(tile_rows, 2 * tile_rows - 1)
+
+    def arrive(numbers):
+        for number in numbers:
+            for copy in halos[number]:
+                copy.wait_recv()
+        span = pl.ds(numbers[0] * chunk, len(numbers) * chunk)
+
+        @pl.when(me == 0)
+        def _():
+            ext[pl.ds(0, OWN), span] = jnp.zeros((OWN, len(numbers) * chunk), BF16)
+
+        @pl.when(me == groups - 1)
+        def _():
+            ext[pl.ds(2 * OWN, OWN), span] = jnp.zeros((OWN, len(numbers) * chunk), BF16)
+
+        return jnp.concatenate([ext[pl.ds(0, OWN), span], ext[pl.ds(2 * OWN, OWN), span]], axis=0)
+
+    early = LENGTH - chunk
+    sides = arrive(range(early // chunk))
+    for number in range(LAGS // 2):
+        partial[number] = products(sides, number, 0, early)
+    sides = arrive([early // chunk])
+    for number in range(LAGS // 2):
+        total = partial[number] + products(sides, number, early, chunk)
+        keep(0, number, total[:OWN])
+        keep(2, number, total[OWN:])
+    finish(0, tile_rows)
+    finish(2 * tile_rows - 1, tiles + tile_rows - 1)
+    for pair in halos:
+        for copy in pair:
+            copy.wait_send()
+    pltpu.make_async_copy(out, out_far, store_sem).wait()
 
 
 def body(groups, inner, signal, fan_cut):
-    whole = pl.BlockSpec(memory_space=pltpu.VMEM)
-    arrays = [jnp.asarray(table) for table in tables(groups)]
+    operands = [signal, fan_cut.reshape(OWN, groups), *(jnp.asarray(table) for table in tables(groups))]
+    anywhere = pl.BlockSpec(memory_space=pl.ANY)
     message = pltpu.VMEM((groups, 4, OWN), F32)
-    ext = pl.pallas_call(
+    result = jax.ShapeDtypeStruct((OWN, BAND * LAGS), F32)
+    return pl.pallas_call(
         functools.partial(filter_kernel, groups, inner),
-        out_shape=jax.ShapeDtypeStruct((3 * OWN, LENGTH), BF16),
-        in_specs=[whole] * (2 + len(arrays)),
-        out_specs=whole,
-        scratch_shapes=[message] * 4 + [pltpu.SemaphoreType.DMA] * 4 + [pltpu.SemaphoreType.DMA((2, 4))] * 2,
+        out_shape=result,
+        in_specs=[anywhere] * len(operands),
+        out_specs=anywhere,
+        scratch_shapes=[pltpu.VMEM(array.shape, array.dtype) for array in operands]
+        + [pltpu.SemaphoreType.DMA((len(operands) + 1,))]
+        + [message] * 4 + [pltpu.SemaphoreType.DMA] * 4 + [pltpu.SemaphoreType.DMA((2, 4))] * 2
+        + [
+            pltpu.VMEM((3 * OWN, LENGTH), BF16),
+            pltpu.VMEM((LAGS * OWN, LENGTH), BF16),
+            pltpu.VMEM((LAGS // 2, 2 * OWN, 2 * OWN), F32),
+            pltpu.VMEM((3 * OWN * LAGS, OWN), F32),
+            pltpu.VMEM(result.shape, F32),
+            pltpu.SemaphoreType.DMA,
+        ],
         compiler_params=pltpu.CompilerParams(
-            collective_id=0, has_side_effects=True, vmem_limit_bytes=40 * 2**20
+            collective_id=0, has_side_effects=True, vmem_limit_bytes=56 * 2**20
         ),
-        name="fan_filter",
-    )(signal, fan_cut.reshape(OWN, groups), *arrays)
-    return pl.pallas_call(
-        correlate_kernel,
-        out_shape=jax.ShapeDtypeStruct((OWN, BAND * LAGS), F32),
-        in_specs=[whole],
-        out_specs=whole,
-        scratch_shapes=[pltpu.VMEM((3 * OWN * LAGS, OWN), F32)],
-        compiler_params=pltpu.CompilerParams(vmem_limit_bytes=40 * 2**20),
-        name="correlate",
-    )(ext)
+        name="fan_filter_correlate",
+    )(*operands)
 
 
 def solution(mesh):

time: 51.9 us -> 41.1 us (0.79)
  local copies, waits for them, and re-layouts: 8.85 us -> 3.11 us
  Pallas kernels: 42.6 us -> 37.8 us
    unnamed x18 -> x1, local copies, waits for them, and re-layouts: 8.85 us -> 3.11 us
    pallas_call x1 -> x0, Pallas kernels: 4.59 us -> none  [body(): pl.pallas_call(correlate_kernel, out_shape=jax.ShapeDtypeStruct((OWN, BAN...]
where the time goes in v1:
time: 41.1 us; the launch traced here: 40.9 us
  Pallas kernels  37.8 us (92%)
  local copies, waits for them, and re-layouts  3.11 us (8%)
    pallas_call x1, Pallas kernels, body(): pl.pallas_call(functools.partial(filter_kernel, groups, inner), out_shape...  37.8 us
    unnamed x1, local copies, waits for them, and re-layouts  3.11 us

profile of v1, /device:TPU:1, one launch (start us, length us, event | category | flops | bytes accessed | tf_op | source)
XLA Modules:
  0.0 40.9 jit_solution(1004715865478445134)
XLA Ops:
  0.0 37.8 %fan_filter_correlate.1 = f32[128,4096]{1,0:T(8,128)} custom-call(f32[128,1024]{1,0:T(8,128)} %signal_far.1, s32[128,128]{1,0:T(8,128)} %bitcast.1, bf16[2,512,1024]{2,1,0:T(8,128)(2,1)} %constant.6.clone.time_far, bf16[4,256,256]{2,1,0:T(8,128)(2,1)} %constant.7.clone.wide_far, f32[2,128,128]{2,1,0:T(8,128)} %constant.8.clone.twist_far), custom_call_target="tpu_custom_call" | custom-call | tf_op jit(solution)/shard_map/fan_filter_correlate/pallas_call | solution.py:299
  37.8 3.1 %copy.7 = f32[128,4096]{1,0:T(8,128)} copy(f32[128,4096]{1,0:T(8,128)} %fan_filter_correlate.1) | data formatting | bytes 4194304

commit v2 on v1

--- a/solution.py
+++ b/solution.py
@@ -70,14 +70,31 @@
     return jnp.maximum(cut.astype(F32), mirrored).T
 
 
+TILES = BAND * LAGS // OWN
+TILE_ROWS = OWN // 8
+
+
+def finish(lagged, out, first, last):
+    lane = lax.broadcasted_iota(jnp.int32, (8, OWN), 1)
+    odd = [(lane // step) % 2 == 1 for step in (1, 2, 4)]
+    for tile in range(first, last):
+        rows = [lagged[pl.ds(tile * OWN + 8 * number, 8), :] for number in range(TILE_ROWS + 14)]
+        for bit in range(3):
+            gap = 2 << bit
+            rows = [jnp.where(odd[bit], rows[spot + gap], rows[spot]) for spot in range(len(rows) - gap)]
+        turned = jnp.concatenate(rows, axis=0).T
+        for group in range(max(0, tile - TILES + 1), min(TILE_ROWS, tile + 1)):
+            out[pl.ds(8 * group, 8), pl.ds((tile - group) * OWN, OWN)] = turned[8 * group:8 * group + 8]
+
+
 def filter_kernel(
     groups, inner,
     signal_far, cut_far, time_far, wide_far, twist_far,
-    out_far,
+    lagged, out,
     signal, cut, time, wide_all, twist, load_sems,
     out_first, in_first, out_second, in_second,
     send_first, recv_first, send_second, recv_second, send_halo, recv_halo,
-    ext, lags, partial, lagged, out, store_sem,
+    ext, lags, partial,
 ):
     outer_at, inner_at = lax.axis_index("cx"), lax.axis_index("cy")
     me = outer_at * inner + inner_at
@@ -233,30 +250,10 @@
             begin = block * OWN * LAGS + 2 * number + side
             lagged[pl.ds(begin, OWN, stride=LAGS), :] = values[:, side * OWN:(side + 1) * OWN]
 
-    lane = lax.broadcasted_iota(jnp.int32, (8, OWN), 1)
-    odd = [(lane // step) % 2 == 1 for step in (1, 2, 4)]
-    tiles = BAND * LAGS // OWN
-    tile_rows = OWN // 8
-
-    def finish(first, last):
-        for tile in range(first, last):
-            rows = [lagged[pl.ds(tile * OWN + 8 * number, 8), :] for number in range(tile_rows + 14)]
-            for bit in range(3):
-                gap = 2 << bit
-                rows = [jnp.where(odd[bit], rows[spot + gap], rows[spot]) for spot in range(len(rows) - gap)]
-            turned = jnp.concatenate(rows, axis=0).T
-            for group in range(max(0, tile - tiles + 1), min(tile_rows, tile + 1)):
-                out[pl.ds(8 * group, 8), pl.ds((tile - group) * OWN, OWN)] = turned[8 * group:8 * group + 8]
-        for group in range(tile_rows):
-            begin, end = max(0, first - group), min(tiles, last - group)
-            if begin < end:
-                place = (pl.ds(8 * group, 8), pl.ds(begin * OWN, (end - begin) * OWN))
-                pltpu.make_async_copy(out.at[place], out_far.at[place], store_sem).start()
-
     middle = ext[pl.ds(OWN, OWN), :]
     for number in range(LAGS // 2):
         keep(1, number, products(middle, number, 0, LENGTH))
-    finish(tile_rows, 2 * tile_rows - 1)
+    finish(lagged, out, TILE_ROWS, 2 * TILE_ROWS - 1)
 
     def arrive(numbers):
         for number in numbers:
@@ -283,24 +280,36 @@
         total = partial[number] + products(sides, number, early, chunk)
         keep(0, number, total[:OWN])
         keep(2, number, total[OWN:])
-    finish(0, tile_rows)
-    finish(2 * tile_rows - 1, tiles + tile_rows - 1)
     for pair in halos:
         for copy in pair:
             copy.wait_send()
+
+
+def write_kernel(lagged, own_out, out_far, out, store_sem):
+    def store(source, first, last):
+        for group in range(TILE_ROWS):
+            begin, end = max(0, first - group), min(TILES, last - group)
+            if begin < end:
+                place = (pl.ds(8 * group, 8), pl.ds(begin * OWN, (end - begin) * OWN))
+                pltpu.make_async_copy(source.at[place], out_far.at[place], store_sem).start()
+
+    store(own_out, TILE_ROWS, 2 * TILE_ROWS - 1)
+    for first, last in ((0, TILE_ROWS), (2 * TILE_ROWS - 1, TILES + TILE_ROWS - 1)):
+        finish(lagged, out, first, last)
+        store(out, first, last)
     pltpu.make_async_copy(out, out_far, store_sem).wait()
 
 
 def body(groups, inner, signal, fan_cut):
     operands = [signal, fan_cut.reshape(OWN, groups), *(jnp.asarray(table) for table in tables(groups))]
-    anywhere = pl.BlockSpec(memory_space=pl.ANY)
+    operands = [pltpu.with_memory_space_constraint(array, pltpu.HBM) for array in operands]
+    far = pl.BlockSpec(memory_space=pltpu.HBM)
     message = pltpu.VMEM((groups, 4, OWN), F32)
-    result = jax.ShapeDtypeStruct((OWN, BAND * LAGS), F32)
-    return pl.pallas_call(
+    lagged, own_out = pl.pallas_call(
         functools.partial(filter_kernel, groups, inner),
-        out_shape=result,
-        in_specs=[anywhere] * len(operands),
-        out_specs=anywhere,
+        out_shape=(pltpu.VMEM((3 * OWN * LAGS, OWN), F32), pltpu.VMEM((OWN, BAND * LAGS), F32)),
+        in_specs=[far] * len(operands),
+        out_specs=(pl.BlockSpec(memory_space=pltpu.VMEM),) * 2,
         scratch_shapes=[pltpu.VMEM(array.shape, array.dtype) for array in operands]
         + [pltpu.SemaphoreType.DMA((len(operands) + 1,))]
         + [message] * 4 + [pltpu.SemaphoreType.DMA] * 4 + [pltpu.SemaphoreType.DMA((2, 4))] * 2
@@ -308,15 +317,22 @@
             pltpu.VMEM((3 * OWN, LENGTH), BF16),
             pltpu.VMEM((LAGS * OWN, LENGTH), BF16),
             pltpu.VMEM((LAGS // 2, 2 * OWN, 2 * OWN), F32),
-            pltpu.VMEM((3 * OWN * LAGS, OWN), F32),
-            pltpu.VMEM(result.shape, F32),
-            pltpu.SemaphoreType.DMA,
         ],
         compiler_params=pltpu.CompilerParams(
-            collective_id=0, has_side_effects=True, vmem_limit_bytes=56 * 2**20
+            collective_id=0, has_side_effects=True, vmem_limit_bytes=40 * 2**20
         ),
-        name="fan_filter_correlate",
+        name="fan_filter_products",
     )(*operands)
+    lagged, own_out = (pltpu.with_memory_space_constraint(array, pltpu.VMEM) for array in (lagged, own_out))
+    return pl.pallas_call(
+        write_kernel,
+        out_shape=jax.ShapeDtypeStruct((OWN, BAND * LAGS), F32),
+        in_specs=[pl.BlockSpec(memory_space=pltpu.VMEM)] * 2,
+        out_specs=far,
+        scratch_shapes=[pltpu.VMEM((OWN, BAND * LAGS), F32), pltpu.SemaphoreType.DMA],
+        compiler_params=pltpu.CompilerParams(vmem_limit_bytes=20 * 2**20),
+        name="correlation_rows",
+    )(lagged, own_out)
 
 
 def solution(mesh):

time: 41.1 us -> 37.9 us (0.922)
  local copies, waits for them, and re-layouts: 3.11 us -> 0 us
    unnamed x1 -> x0, local copies, waits for them, and re-layouts: 3.11 us -> none
    pallas_call x0 -> x1, Pallas kernels: none -> 1.42 us  [body(): pl.pallas_call(write_kernel, out_shape=jax.ShapeDtypeStruct((OWN, BAND *...]
    pallas_call x1, Pallas kernels: 37.8 us -> 36.4 us  [body(): pl.pallas_call(functools.partial(filter_kernel, groups, inner), out_shape...]
where the time goes in v2:
time: 37.9 us; the launch traced here: 37.8 us
  Pallas kernels  37.8 us (100%)
    pallas_call x1, Pallas kernels, body(): pl.pallas_call(functools.partial(filter_kernel, groups, inner), out_shape...  36.4 us
    pallas_call x1, Pallas kernels, body(): pl.pallas_call(write_kernel, out_shape=jax.ShapeDtypeStruct((OWN, BAND *...  1.42 us

profile of v2, /device:TPU:1, one launch (start us, length us, event | category | flops | bytes accessed | tf_op | source)
XLA Modules:
  0.0 37.8 jit_solution(14688455037874139667)
XLA Ops:
  0.0 36.4 %fan_filter_products.1 = (f32[6144,128]{1,0:T(8,128)S(1)}, f32[128,4096]{1,0:T(8,128)S(1)}) custom-call(f32[128,1024]{1,0:T(8,128)} %signal_far.1, s32[128,128]{1,0:T(8,128)} %bitcast.1, bf16[2,512,1024]{2,1,0:T(8,128)(2,1)} %constant.6.clone.time_far, bf16[4,256,256]{2,1,0:T(8,128)(2,1)} %constant.7.clone.wide_far, f32[2,128,128]{2,1,0:T(8,128)} %constant.8.clone.twist_far), custom_call_target="tpu_custom_call" | custom-call | tf_op jit(solution)/shard_map/fan_filter_products/pallas_call | solution.py:308
  36.4 1.4 %correlation_rows.1 = f32[128,4096]{1,0:T(8,128)} custom-call(f32[6144,128]{1,0:T(8,128)S(1)} %get-tuple-element.7.lagged, f32[128,4096]{1,0:T(8,128)S(1)} %get-tuple-element.8.own_out), custom_call_target="tpu_custom_call" | custom-call | tf_op jit(solution)/shard_map/correlation_rows/pallas_call | solution.py:327

commit v3 on v2

--- a/solution.py
+++ b/solution.py
@@ -29,13 +29,16 @@
     angle = 2.0 * math.pi / LENGTH * (bin_index[:, None] * np.arange(LENGTH)[None, :] % LENGTH)
     pairs = np.stack([np.cos(angle), -np.sin(angle)], axis=1).reshape(groups, 2, 2, LENGTH)
     time = pairs.transpose(0, 2, 1, 3).reshape(2 * BINS, LENGTH)
+    time[2] = np.cos(math.pi * np.arange(LENGTH))
+    angle = 2.0 * math.pi / LENGTH * ((bin_index + BINS)[:, None] * np.arange(LENGTH)[None, :] % LENGTH)
+    upper = np.concatenate([np.cos(angle), -np.sin(angle)])
     index = np.arange(groups)
     angle = 2.0 * math.pi / groups * (index[:, None] * index[None, :] % groups)
     re, im = np.cos(angle), -np.sin(angle)
     wide = np.block([[re, -im], [im, re]])
     angle = 2.0 * math.pi / (groups * OWN) * (index[:, None] * index[None, :])
     twist = np.stack([np.cos(angle), np.sin(angle)]).astype(np.float32)
-    return np.stack(halves(time)), np.stack([*halves(wide), *halves(wide.T)]), twist
+    return np.stack(halves(time)), np.stack([*halves(wide), *halves(wide.T)]), twist, np.stack(halves(upper))
 
 
 def dot(left, right, dims=((1,), (0,))):
@@ -89,12 +92,12 @@
 
 def filter_kernel(
     groups, inner,
-    signal_far, cut_far, time_far, wide_far, twist_far,
+    signal_far, cut_far, time_far, wide_far, twist_far, upper_far,
     lagged, out,
-    signal, cut, time, wide_all, twist, load_sems,
+    signal, cut, time, wide_all, twist, upper, load_sems,
     out_first, in_first, out_second, in_second,
-    send_first, recv_first, send_second, recv_second, send_halo, recv_halo,
-    ext, lags, partial,
+    send_first, recv_first, send_second, recv_second, send_upper, recv_upper, send_lower, recv_lower,
+    own_bins, upper_out, upper_in, upper_sides, lower_out, lower_in, ext, lags, sides,
 ):
     outer_at, inner_at = lax.axis_index("cx"), lax.axis_index("cy")
     me = outer_at * inner + inner_at
@@ -128,9 +131,9 @@
         near(0, 0, every[:-1])
 
     pairs = ((signal_far, signal), (time_far.at[0], time.at[0]), (time_far.at[1], time.at[1]),
-             (cut_far, cut), (wide_far, wide_all), (twist_far, twist))
+             (cut_far, cut), (wide_far, wide_all), (twist_far, twist), (upper_far, upper))
     loads = [pltpu.make_async_copy(far, near, load_sems.at[number]) for number, (far, near) in enumerate(pairs)]
-    for load in loads:
+    for load in loads[:-1]:
         load.start()
 
     barrier = pltpu.get_barrier_semaphore()
@@ -149,6 +152,7 @@
     spectrum = (wide_sum[:, :OWN] + wide_sum[:, OWN:]) + dot(time_low[...], own_high, ((1,), (1,)))
     out_first[...] = spectrum.reshape(groups, 4, OWN)
 
+    loads[-1].start()
     pl.semaphore_wait(barrier, groups - 1)
 
     def exchange(outgoing, incoming, send_sem, recv_sem):
@@ -179,6 +183,26 @@
     exchange(out_first, in_first, send_first, recv_first)
     for load in loads[3:]:
         load.wait()
+    lane = lax.broadcasted_iota(jnp.int32, (OWN, 2 * BINS), 1)
+    own_bins[...] = spectrum.T * jnp.where((lane == 0) | (lane == 2), 1.0 / LENGTH, 2.0 / LENGTH)
+    upper_sum = dot(both, upper[0], ((1,), (1,)))
+    upper_sum = (upper_sum[:OWN] + upper_sum[OWN:]) + dot(own_high, upper[1], ((1,), (1,)))
+    upper_out[...] = (upper_sum * (2.0 / LENGTH)).astype(BF16)
+
+    def to_sides(outgoing, incoming, send_sems, recv_sems, rows):
+        copies = [
+            pltpu.make_async_remote_copy(
+                src_ref=outgoing.at[rows], dst_ref=incoming.at[side, rows],
+                send_sem=send_sems.at[side], recv_sem=recv_sems.at[side],
+                device_id=at(peer(1 if side == 0 else groups - 1)), device_id_type=MESH,
+            )
+            for side in range(2)
+        ]
+        for copy in copies:
+            copy.start()
+        return copies
+
+    early = to_sides(upper_out, upper_in, send_upper, recv_upper, pl.ds(0, OWN))
     cut_least = least_cut(cut[...])
     wide = (wide_all[0], wide_all[1])
     flip = (wide_all[2], wide_all[3])
@@ -186,6 +210,7 @@
     settle(out_first, in_first, send_first, recv_first)
 
     rows = [in_first[:, part, :] for part in range(4)]
+    rows[2] = rows[2] * jnp.where(me == 0, 0.0, 1.0)
     value = dot_three(wide, split(join(*rows)))
     re_a, re_b, im_a, im_b = blocks(value)
     value = join(
@@ -209,80 +234,68 @@
         out_second[:, part, :] = block
 
     exchange(out_second, in_second, send_second, recv_second)
+    for copy in early:
+        copy.wait_recv()
+    bins = upper_in[...].reshape(2 * OWN, 2 * BINS)
+    upper_sides[...] = dot(bins, upper[0]) + dot(bins, upper[1])
     settle(out_second, in_second, send_second, recv_second)
 
-    back_high, back_low = split(in_second[...].reshape(4 * groups, OWN).T)
+    back = in_second[...].reshape(4 * groups, OWN).T
+    lower_out[...] = (own_bins[...] + back).astype(BF16)
+    half = OWN // 2
+    late = [
+        to_sides(lower_out, lower_in, send_lower.at[part], recv_lower.at[part], pl.ds(part * half, half))
+        for part in range(2)
+    ]
+    back_high, back_low = split(back)
     both = jnp.concatenate([back_high, back_low], axis=0)
-    halos = []
     chunk = 256
     for number in range(LENGTH // chunk):
         span = pl.ds(number * chunk, chunk)
         high, low = time_high[:, span], time_low[:, span]
         sums = dot(both, high)
         rejected = (sums[:OWN] + sums[OWN:]) + dot(back_high, low)
-        ext[pl.ds(OWN, OWN), span] = (signal[:, span] + rejected).astype(BF16)
-        source = ext.at[pl.ds(OWN, OWN), span]
-        halos.append((
-            pltpu.make_async_remote_copy(
-                src_ref=source, dst_ref=ext.at[pl.ds(0, OWN), span],
-                send_sem=send_halo.at[0, number], recv_sem=recv_halo.at[0, number],
-                device_id=at(peer(1)), device_id_type=MESH,
-            ),
-            pltpu.make_async_remote_copy(
-                src_ref=source, dst_ref=ext.at[pl.ds(2 * OWN, OWN), span],
-                send_sem=send_halo.at[1, number], recv_sem=recv_halo.at[1, number],
-                device_id=at(peer(groups - 1)), device_id_type=MESH,
-            ),
-        ))
-        for copy in halos[-1]:
-            copy.start()
-    own = ext[pl.ds(OWN, OWN), :] * jnp.asarray(1.0 / math.sqrt(LENGTH), BF16)
+        ext[:, span] = (signal[:, span] + rejected).astype(BF16)
+    own = ext[...] * jnp.asarray(1.0 / math.sqrt(LENGTH), BF16)
     for lag in range(LAGS):
         lags[pl.ds(lag * OWN, OWN), :] = own if lag == 0 else jnp.concatenate(
             [jnp.zeros((OWN, lag), BF16), own[:, :LENGTH - lag]], axis=1
         )
 
-    def products(rows, number, begin, length):
-        return dot(rows, lags[pl.ds(number * 2 * OWN, 2 * OWN), begin:begin + length], ((1,), (1,)))
-
-    def keep(block, number, values):
+    def products(rows, number):
+        return dot(rows, lags[pl.ds(number * 2 * OWN, 2 * OWN), :], ((1,), (1,)))
+
+    def keep(first_row, number, values):
         for side in range(2):
-            begin = block * OWN * LAGS + 2 * number + side
-            lagged[pl.ds(begin, OWN, stride=LAGS), :] = values[:, side * OWN:(side + 1) * OWN]
-
-    middle = ext[pl.ds(OWN, OWN), :]
+            begin = first_row * LAGS + 2 * number + side
+            lagged[pl.ds(begin, values.shape[0], stride=LAGS), :] = values[:, side * OWN:(side + 1) * OWN]
+
+    middle = ext[...]
     for number in range(LAGS // 2):
-        keep(1, number, products(middle, number, 0, LENGTH))
+        keep(OWN, number, products(middle, number))
     finish(lagged, out, TILE_ROWS, 2 * TILE_ROWS - 1)
 
-    def arrive(numbers):
-        for number in numbers:
-            for copy in halos[number]:
-                copy.wait_recv()
-        span = pl.ds(numbers[0] * chunk, len(numbers) * chunk)
-
-        @pl.when(me == 0)
-        def _():
-            ext[pl.ds(0, OWN), span] = jnp.zeros((OWN, len(numbers) * chunk), BF16)
-
-        @pl.when(me == groups - 1)
-        def _():
-            ext[pl.ds(2 * OWN, OWN), span] = jnp.zeros((OWN, len(numbers) * chunk), BF16)
-
-        return jnp.concatenate([ext[pl.ds(0, OWN), span], ext[pl.ds(2 * OWN, OWN), span]], axis=0)
-
-    early = LENGTH - chunk
-    sides = arrive(range(early // chunk))
-    for number in range(LAGS // 2):
-        partial[number] = products(sides, number, 0, early)
-    sides = arrive([early // chunk])
-    for number in range(LAGS // 2):
-        total = partial[number] + products(sides, number, early, chunk)
-        keep(0, number, total[:OWN])
-        keep(2, number, total[OWN:])
-    for pair in halos:
-        for copy in pair:
-            copy.wait_send()
+    row = lax.broadcasted_iota(jnp.int32, (OWN, chunk), 0)
+    inside = jnp.where(row < half, (me > 0).astype(F32), (me < groups - 1).astype(F32))
+    for part in range(2):
+        for copy in late[part]:
+            copy.wait_recv()
+        rows = pl.ds(part * half, half)
+        bins = jnp.concatenate([lower_in[0, rows, :], lower_in[1, rows, :]], axis=0)
+        for number in range(LENGTH // chunk):
+            span = pl.ds(number * chunk, chunk)
+            upper_part = jnp.concatenate(
+                [upper_sides[rows, span], upper_sides[pl.ds(OWN + part * half, half), span]], axis=0
+            )
+            value = dot(bins, time_high[:, span]) + dot(bins, time_low[:, span]) + upper_part
+            sides[:, span] = (value * inside).astype(BF16)
+        middle = sides[...]
+        for number in range(LAGS // 2):
+            values = products(middle, number)
+            keep(part * half, number, values[:half])
+            keep(2 * OWN + part * half, number, values[half:])
+    for copy in early + late[0] + late[1]:
+        copy.wait_send()
 
 
 def write_kernel(lagged, own_out, out_far, out, store_sem):
@@ -312,11 +325,17 @@
         out_specs=(pl.BlockSpec(memory_space=pltpu.VMEM),) * 2,
         scratch_shapes=[pltpu.VMEM(array.shape, array.dtype) for array in operands]
         + [pltpu.SemaphoreType.DMA((len(operands) + 1,))]
-        + [message] * 4 + [pltpu.SemaphoreType.DMA] * 4 + [pltpu.SemaphoreType.DMA((2, 4))] * 2
+        + [message] * 4 + [pltpu.SemaphoreType.DMA] * 4 + [pltpu.SemaphoreType.DMA((2,))] * 2 + [pltpu.SemaphoreType.DMA((2, 2))] * 2
         + [
-            pltpu.VMEM((3 * OWN, LENGTH), BF16),
+            pltpu.VMEM((OWN, 2 * BINS), F32),
+            pltpu.VMEM((OWN, 2 * BINS), BF16),
+            pltpu.VMEM((2, OWN, 2 * BINS), BF16),
+            pltpu.VMEM((2 * OWN, LENGTH), F32),
+            pltpu.VMEM((OWN, 2 * BINS), BF16),
+            pltpu.VMEM((2, OWN, 2 * BINS), BF16),
+            pltpu.VMEM((OWN, LENGTH), BF16),
             pltpu.VMEM((LAGS * OWN, LENGTH), BF16),
-            pltpu.VMEM((LAGS // 2, 2 * OWN, 2 * OWN), F32),
+            pltpu.VMEM((OWN, LENGTH), BF16),
         ],
         compiler_params=pltpu.CompilerParams(
             collective_id=0, has_side_effects=True, vmem_limit_bytes=40 * 2**20

time: 37.9 us -> 37.3 us (0.984)
  Pallas kernels: 37.8 us -> 37.2 us
    pallas_call x1, Pallas kernels: 36.4 us -> 35.8 us  [body(): pl.pallas_call(functools.partial(filter_kernel, groups, inner), out_shape...]
where the time goes in v3:
time: 37.3 us; the launch traced here: 37.2 us
  Pallas kernels  37.2 us (100%)
    pallas_call x1, Pallas kernels, body(): pl.pallas_call(functools.partial(filter_kernel, groups, inner), out_shape...  35.8 us
    pallas_call x1, Pallas kernels, body(): pl.pallas_call(write_kernel, out_shape=jax.ShapeDtypeStruct((OWN, BAND *...  1.42 us

profile of v3, /device:TPU:1, one launch (start us, length us, event | category | flops | bytes accessed | tf_op | source)
XLA Modules:
  0.0 37.2 jit_solution(5984685331815222202)
XLA Ops:
  0.0 35.8 %fan_filter_products.1 = (f32[6144,128]{1,0:T(8,128)S(1)}, f32[128,4096]{1,0:T(8,128)S(1)}) custom-call(f32[128,1024]{1,0:T(8,128)} %signal_far.1, s32[128,128]{1,0:T(8,128)} %bitcast.1, bf16[2,512,1024]{2,1,0:T(8,128)(2,1)} %constant.8.clone.time_far, bf16[4,256,256]{2,1,0:T(8,128)(2,1)} %constant.9.clone.wide_far, ...), custom_call_target="tpu_custom_call" | custom-call | tf_op jit(solution)/shard_map/fan_filter_products/pallas_call | solution.py:321
  35.8 1.4 %correlation_rows.1 = f32[128,4096]{1,0:T(8,128)} custom-call(f32[6144,128]{1,0:T(8,128)S(1)} %get-tuple-element.7.lagged, f32[128,4096]{1,0:T(8,128)S(1)} %get-tuple-element.8.own_out), custom_call_target="tpu_custom_call" | custom-call | tf_op jit(solution)/shard_map/correlation_rows/pallas_call | solution.py:346

commit v4 on v3

--- a/solution.py
+++ b/solution.py
@@ -28,8 +28,8 @@
     bin_index = np.arange(BINS, dtype=np.int64)
     angle = 2.0 * math.pi / LENGTH * (bin_index[:, None] * np.arange(LENGTH)[None, :] % LENGTH)
     pairs = np.stack([np.cos(angle), -np.sin(angle)], axis=1).reshape(groups, 2, 2, LENGTH)
-    time = pairs.transpose(0, 2, 1, 3).reshape(2 * BINS, LENGTH)
-    time[2] = np.cos(math.pi * np.arange(LENGTH))
+    time = pairs.transpose(2, 1, 0, 3).reshape(2 * BINS, LENGTH)
+    time[2 * groups] = np.cos(math.pi * np.arange(LENGTH))
     angle = 2.0 * math.pi / LENGTH * ((bin_index + BINS)[:, None] * np.arange(LENGTH)[None, :] % LENGTH)
     upper = np.concatenate([np.cos(angle), -np.sin(angle)])
     index = np.arange(groups)
@@ -75,6 +75,7 @@
 
 TILES = BAND * LAGS // OWN
 TILE_ROWS = OWN // 8
+PACK = 16
 
 
 def finish(lagged, out, first, last):
@@ -93,11 +94,11 @@
 def filter_kernel(
     groups, inner,
     signal_far, cut_far, time_far, wide_far, twist_far, upper_far,
-    lagged, out,
+    lagged,
     signal, cut, time, wide_all, twist, upper, load_sems,
     out_first, in_first, out_second, in_second,
-    send_first, recv_first, send_second, recv_second, send_upper, recv_upper, send_lower, recv_lower,
-    own_bins, upper_out, upper_in, upper_sides, lower_out, lower_in, ext, lags, sides,
+    send_first, recv_first, send_second, recv_second, send_upper, recv_upper,
+    upper_out, upper_in, upper_sides, packed, ext, lags,
 ):
     outer_at, inner_at = lax.axis_index("cx"), lax.axis_index("cy")
     me = outer_at * inner + inner_at
@@ -150,7 +151,8 @@
     wide_sum = dot(time_high[...], both, ((1,), (1,)))
     loads[2].wait()
     spectrum = (wide_sum[:, :OWN] + wide_sum[:, OWN:]) + dot(time_low[...], own_high, ((1,), (1,)))
-    out_first[...] = spectrum.reshape(groups, 4, OWN)
+    for part in range(4):
+        out_first[:, part, :] = spectrum[part * OWN:(part + 1) * OWN]
 
     loads[-1].start()
     pl.semaphore_wait(barrier, groups - 1)
@@ -183,26 +185,20 @@
     exchange(out_first, in_first, send_first, recv_first)
     for load in loads[3:]:
         load.wait()
-    lane = lax.broadcasted_iota(jnp.int32, (OWN, 2 * BINS), 1)
-    own_bins[...] = spectrum.T * jnp.where((lane == 0) | (lane == 2), 1.0 / LENGTH, 2.0 / LENGTH)
     upper_sum = dot(both, upper[0], ((1,), (1,)))
     upper_sum = (upper_sum[:OWN] + upper_sum[OWN:]) + dot(own_high, upper[1], ((1,), (1,)))
     upper_out[...] = (upper_sum * (2.0 / LENGTH)).astype(BF16)
 
-    def to_sides(outgoing, incoming, send_sems, recv_sems, rows):
-        copies = [
-            pltpu.make_async_remote_copy(
-                src_ref=outgoing.at[rows], dst_ref=incoming.at[side, rows],
-                send_sem=send_sems.at[side], recv_sem=recv_sems.at[side],
-                device_id=at(peer(1 if side == 0 else groups - 1)), device_id_type=MESH,
-            )
-            for side in range(2)
-        ]
-        for copy in copies:
-            copy.start()
-        return copies
-
-    early = to_sides(upper_out, upper_in, send_upper, recv_upper, pl.ds(0, OWN))
+    early = [
+        pltpu.make_async_remote_copy(
+            src_ref=upper_out, dst_ref=upper_in.at[side],
+            send_sem=send_upper.at[side], recv_sem=recv_upper.at[side],
+            device_id=at(peer(1 if side == 0 else groups - 1)), device_id_type=MESH,
+        )
+        for side in range(2)
+    ]
+    for copy in early:
+        copy.start()
     cut_least = least_cut(cut[...])
     wide = (wide_all[0], wide_all[1])
     flip = (wide_all[2], wide_all[3])
@@ -210,8 +206,7 @@
     settle(out_first, in_first, send_first, recv_first)
 
     rows = [in_first[:, part, :] for part in range(4)]
-    rows[2] = rows[2] * jnp.where(me == 0, 0.0, 1.0)
-    value = dot_three(wide, split(join(*rows)))
+    value = dot_three(wide, split(join(rows[0], rows[1], rows[2] * jnp.where(me == 0, 0.0, 1.0), rows[3])))
     re_a, re_b, im_a, im_b = blocks(value)
     value = join(
         re_a * cosine + im_a * sine, im_a * cosine - re_a * sine,
@@ -231,85 +226,63 @@
     )
     value = dot_three(flip, split(value))
     for part, block in enumerate(blocks(value)):
-        out_second[:, part, :] = block
+        weight = 2.0 / LENGTH if part % 2 else jnp.where(me == 0, 1.0 / LENGTH, 2.0 / LENGTH)
+        kept = rows[part] * weight + block
+        for first, array in (
+            (PACK, block), (PACK + 4, block - block.astype(BF16).astype(F32)), (2 * PACK + 8, kept), (12, kept),
+        ):
+            packed[pl.ds(first + part, groups, stride=PACK), :] = array
+    for first in (PACK + 8, PACK * groups + 12):
+        packed[pl.ds(first, 4), :] = jnp.zeros((4, OWN), F32)
+    out_second[...] = packed[pl.ds(PACK, PACK * groups), :].astype(BF16).reshape(groups, PACK, OWN)
 
     exchange(out_second, in_second, send_second, recv_second)
     for copy in early:
         copy.wait_recv()
     bins = upper_in[...].reshape(2 * OWN, 2 * BINS)
-    upper_sides[...] = dot(bins, upper[0]) + dot(bins, upper[1])
+    row = lax.broadcasted_iota(jnp.int32, (2 * OWN, LENGTH), 0)
+    inside = jnp.where(row < OWN, (me > 0).astype(F32), (me < groups - 1).astype(F32))
+    upper_sides[...] = (dot(bins, upper[0]) + dot(bins, upper[1])) * inside
     settle(out_second, in_second, send_second, recv_second)
 
-    back = in_second[...].reshape(4 * groups, OWN).T
-    lower_out[...] = (own_bins[...] + back).astype(BF16)
-    half = OWN // 2
-    late = [
-        to_sides(lower_out, lower_in, send_lower.at[part], recv_lower.at[part], pl.ds(part * half, half))
-        for part in range(2)
-    ]
-    back_high, back_low = split(back)
-    both = jnp.concatenate([back_high, back_low], axis=0)
+    packed[pl.ds(0, PACK * groups), :] = in_second[...].astype(F32).reshape(PACK * groups, OWN)
+
+    def turn(*firsts):
+        parts = [[packed[pl.ds(first + part, groups, stride=PACK), :] for first in firsts] for part in range(4)]
+        return jnp.concatenate([sum(part[1:], part[0]).T for part in parts], axis=1)
+
+    back_high, back_low = split(turn(0, 4))
+    all_bins = jnp.concatenate([back_high, back_low, turn(8).astype(BF16), turn(12).astype(BF16)], axis=0)
     chunk = 256
     for number in range(LENGTH // chunk):
         span = pl.ds(number * chunk, chunk)
-        high, low = time_high[:, span], time_low[:, span]
-        sums = dot(both, high)
-        rejected = (sums[:OWN] + sums[OWN:]) + dot(back_high, low)
-        ext[:, span] = (signal[:, span] + rejected).astype(BF16)
-    own = ext[...] * jnp.asarray(1.0 / math.sqrt(LENGTH), BF16)
+        sums = dot(all_bins, time_high[:, span])
+        rejected = (sums[:OWN] + sums[OWN:2 * OWN]) + dot(back_high, time_low[:, span])
+        ext[pl.ds(OWN, OWN), span] = (signal[:, span] + rejected).astype(BF16)
+        ext[pl.ds(0, OWN), span] = (upper_sides[pl.ds(0, OWN), span] + sums[2 * OWN:3 * OWN]).astype(BF16)
+        ext[pl.ds(2 * OWN, OWN), span] = (upper_sides[pl.ds(OWN, OWN), span] + sums[3 * OWN:]).astype(BF16)
+    own = ext[pl.ds(OWN, OWN), :] * jnp.asarray(1.0 / math.sqrt(LENGTH), BF16)
     for lag in range(LAGS):
         lags[pl.ds(lag * OWN, OWN), :] = own if lag == 0 else jnp.concatenate(
             [jnp.zeros((OWN, lag), BF16), own[:, :LENGTH - lag]], axis=1
         )
 
-    def products(rows, number):
-        return dot(rows, lags[pl.ds(number * 2 * OWN, 2 * OWN), :], ((1,), (1,)))
-
-    def keep(first_row, number, values):
+    everything = ext[...]
+    for number in range(LAGS // 2):
+        values = dot(everything, lags[pl.ds(number * 2 * OWN, 2 * OWN), :], ((1,), (1,)))
         for side in range(2):
-            begin = first_row * LAGS + 2 * number + side
-            lagged[pl.ds(begin, values.shape[0], stride=LAGS), :] = values[:, side * OWN:(side + 1) * OWN]
-
-    middle = ext[...]
-    for number in range(LAGS // 2):
-        keep(OWN, number, products(middle, number))
-    finish(lagged, out, TILE_ROWS, 2 * TILE_ROWS - 1)
-
-    row = lax.broadcasted_iota(jnp.int32, (OWN, chunk), 0)
-    inside = jnp.where(row < half, (me > 0).astype(F32), (me < groups - 1).astype(F32))
-    for part in range(2):
-        for copy in late[part]:
-            copy.wait_recv()
-        rows = pl.ds(part * half, half)
-        bins = jnp.concatenate([lower_in[0, rows, :], lower_in[1, rows, :]], axis=0)
-        for number in range(LENGTH // chunk):
-            span = pl.ds(number * chunk, chunk)
-            upper_part = jnp.concatenate(
-                [upper_sides[rows, span], upper_sides[pl.ds(OWN + part * half, half), span]], axis=0
-            )
-            value = dot(bins, time_high[:, span]) + dot(bins, time_low[:, span]) + upper_part
-            sides[:, span] = (value * inside).astype(BF16)
-        middle = sides[...]
-        for number in range(LAGS // 2):
-            values = products(middle, number)
-            keep(part * half, number, values[:half])
-            keep(2 * OWN + part * half, number, values[half:])
-    for copy in early + late[0] + late[1]:
+            lagged[pl.ds(2 * number + side, 3 * OWN, stride=LAGS), :] = values[:, side * OWN:(side + 1) * OWN]
+    for copy in early:
         copy.wait_send()
 
 
-def write_kernel(lagged, own_out, out_far, out, store_sem):
-    def store(source, first, last):
-        for group in range(TILE_ROWS):
-            begin, end = max(0, first - group), min(TILES, last - group)
-            if begin < end:
-                place = (pl.ds(8 * group, 8), pl.ds(begin * OWN, (end - begin) * OWN))
-                pltpu.make_async_copy(source.at[place], out_far.at[place], store_sem).start()
-
-    store(own_out, TILE_ROWS, 2 * TILE_ROWS - 1)
-    for first, last in ((0, TILE_ROWS), (2 * TILE_ROWS - 1, TILES + TILE_ROWS - 1)):
-        finish(lagged, out, first, last)
-        store(out, first, last)
+def write_kernel(lagged, out_far, out, store_sem):
+    done = 0
+    for last in range(TILE_ROWS + TILES // 4 - 1, TILE_ROWS + TILES, TILES // 4):
+        finish(lagged, out, done, last)
+        done = last
+        columns = pl.ds((last - TILE_ROWS + 1 - TILES // 4) * OWN, TILES // 4 * OWN)
+        pltpu.make_async_copy(out.at[:, columns], out_far.at[:, columns], store_sem).start()
     pltpu.make_async_copy(out, out_far, store_sem).wait()
 
 
@@ -317,41 +290,38 @@
     operands = [signal, fan_cut.reshape(OWN, groups), *(jnp.asarray(table) for table in tables(groups))]
     operands = [pltpu.with_memory_space_constraint(array, pltpu.HBM) for array in operands]
     far = pl.BlockSpec(memory_space=pltpu.HBM)
-    message = pltpu.VMEM((groups, 4, OWN), F32)
-    lagged, own_out = pl.pallas_call(
+    messages = [pltpu.VMEM((groups, 4, OWN), F32)] * 2 + [pltpu.VMEM((groups, PACK, OWN), BF16)] * 2
+    lagged = pl.pallas_call(
         functools.partial(filter_kernel, groups, inner),
-        out_shape=(pltpu.VMEM((3 * OWN * LAGS, OWN), F32), pltpu.VMEM((OWN, BAND * LAGS), F32)),
+        out_shape=pltpu.VMEM((3 * OWN * LAGS, OWN), F32),
         in_specs=[far] * len(operands),
-        out_specs=(pl.BlockSpec(memory_space=pltpu.VMEM),) * 2,
+        out_specs=pl.BlockSpec(memory_space=pltpu.VMEM),
         scratch_shapes=[pltpu.VMEM(array.shape, array.dtype) for array in operands]
         + [pltpu.SemaphoreType.DMA((len(operands) + 1,))]
-        + [message] * 4 + [pltpu.SemaphoreType.DMA] * 4 + [pltpu.SemaphoreType.DMA((2,))] * 2 + [pltpu.SemaphoreType.DMA((2, 2))] * 2
+        + messages + [pltpu.SemaphoreType.DMA] * 4 + [pltpu.SemaphoreType.DMA((2,))] * 2
         + [
-            pltpu.VMEM((OWN, 2 * BINS), F32),
             pltpu.VMEM((OWN, 2 * BINS), BF16),
             pltpu.VMEM((2, OWN, 2 * BINS), BF16),
             pltpu.VMEM((2 * OWN, LENGTH), F32),
-            pltpu.VMEM((OWN, 2 * BINS), BF16),
-            pltpu.VMEM((2, OWN, 2 * BINS), BF16),
-            pltpu.VMEM((OWN, LENGTH), BF16),
+            pltpu.VMEM((PACK * (groups + 2), OWN), F32),
+            pltpu.VMEM((3 * OWN, LENGTH), BF16),
             pltpu.VMEM((LAGS * OWN, LENGTH), BF16),
-            pltpu.VMEM((OWN, LENGTH), BF16),
         ],
         compiler_params=pltpu.CompilerParams(
             collective_id=0, has_side_effects=True, vmem_limit_bytes=40 * 2**20
         ),
         name="fan_filter_products",
     )(*operands)
-    lagged, own_out = (pltpu.with_memory_space_constraint(array, pltpu.VMEM) for array in (lagged, own_out))
+    lagged = pltpu.with_memory_space_constraint(lagged, pltpu.VMEM)
     return pl.pallas_call(
         write_kernel,
         out_shape=jax.ShapeDtypeStruct((OWN, BAND * LAGS), F32),
-        in_specs=[pl.BlockSpec(memory_space=pltpu.VMEM)] * 2,
+        in_specs=[pl.BlockSpec(memory_space=pltpu.VMEM)],
         out_specs=far,
         scratch_shapes=[pltpu.VMEM((OWN, BAND * LAGS), F32), pltpu.SemaphoreType.DMA],
         compiler_params=pltpu.CompilerParams(vmem_limit_bytes=20 * 2**20),
         name="correlation_rows",
-    )(lagged, own_out)
+    )(lagged)
 
 
 def solution(mesh):

time: 37.3 us -> 34.9 us (0.936)
  Pallas kernels: 37.2 us -> 34.8 us
    pallas_call x1, Pallas kernels: 35.8 us -> 32.9 us  [body(): pl.pallas_call(functools.partial(filter_kernel, groups, inner), out_shape...]
    pallas_call x1, Pallas kernels: 1.42 us -> 1.8 us  [body(): pl.pallas_call(write_kernel, out_shape=jax.ShapeDtypeStruct((OWN, BAND *...]
where the time goes in v4:
time: 34.9 us; the launch traced here: 34.8 us
  Pallas kernels  34.8 us (100%)
    pallas_call x1, Pallas kernels, body(): pl.pallas_call(functools.partial(filter_kernel, groups, inner), out_shape...  32.9 us
    pallas_call x1, Pallas kernels, body(): pl.pallas_call(write_kernel, out_shape=jax.ShapeDtypeStruct((OWN, BAND *...  1.8 us

profile of v4, /device:TPU:1, one launch (start us, length us, event | category | flops | bytes accessed | tf_op | source)
XLA Modules:
  0.0 34.8 jit_solution(15238030348749219127)
XLA Ops:
  0.0 32.9 %fan_filter_products.1.lagged = f32[6144,128]{1,0:T(8,128)S(1)} custom-call(f32[128,1024]{1,0:T(8,128)} %signal_far.1, s32[128,128]{1,0:T(8,128)} %bitcast.1, bf16[2,512,1024]{2,1,0:T(8,128)(2,1)} %constant.8.clone.time_far, bf16[4,256,256]{2,1,0:T(8,128)(2,1)} %constant.9.clone.wide_far, f32[2,128,128]{2,1,0:T(8,128)} %constant.10.clone.twist_far, ...), custom_call_target="tpu_custom_call" | custom-call | tf_op jit(solution)/shard_map/fan_filter_products/pallas_call | solution.py:294
  33.0 1.8 %correlation_rows.1 = f32[128,4096]{1,0:T(8,128)} custom-call(f32[6144,128]{1,0:T(8,128)S(1)} %fan_filter_products.1.lagged), custom_call_target="tpu_custom_call" | custom-call | tf_op jit(solution)/shard_map/correlation_rows/pallas_call | solution.py:316

commit v5 on v4

--- a/solution.py
+++ b/solution.py
@@ -112,24 +112,23 @@
     def visit_others(visit):
         high, mid, core = outer_at // 8, lax.rem(outer_at // 2, 4), lax.rem(outer_at, 2)
         top, low = inner_at // 4, lax.rem(inner_at, 4)
-        highs, cores, tops = [8 * high, 8 - 8 * high], [core, 1 - core], [4 * top, 4 - 4 * top]
-
-        def near(mid_step, low_step, combinations):
-            mid_to, low_to = 2 * lax.rem(mid + mid_step, 4), lax.rem(low + low_step, 4)
-            for flip_top, flip_high, flip_core in combinations:
-                visit(highs[flip_high] + mid_to + cores[flip_core], tops[flip_top] + low_to)
-
-        every = [(i, j, k) for i in (1, 0) for j in (1, 0) for k in (1, 0)]
-
-        def far(number):
-            return number + 2 - (number // 2) * (2 * number - 1)
-
-        def block(index, carry):
-            near(far(index // 4), far(lax.rem(index, 4)), every)
+        highs, cores, tops = (8 * high, 8 - 8 * high), (core, 1 - core), (4 * top, 4 - 4 * top)
+        mids = [2 * lax.rem(mid + step, 4) for step in range(4)]
+        lows = [lax.rem(low + step, 4) for step in range(4)]
+        far = ((2, 2), (1, 3), (3, 1), (1, 1), (3, 3), (2, 1), (1, 2), (2, 3), (3, 2))
+        near = ((2, 0), (0, 2), (1, 0), (0, 3), (3, 0), (0, 1), (0, 0))
+
+        def block(index, carry, steps):
+            cx = jnp.where(lax.rem(index // 2, 2) == 0, highs[1], highs[0])
+            cx = cx + jnp.where(lax.rem(index, 2) == 0, cores[1], cores[0])
+            cy = jnp.where(index // 4 == 0, tops[1], tops[0])
+            for mid_step, low_step in steps:
+                visit(cx + mids[mid_step], cy + lows[low_step])
             return carry
 
-        lax.fori_loop(0, 15, block, 0)
-        near(0, 0, every[:-1])
+        lax.fori_loop(0, 8, functools.partial(block, steps=far), 0)
+        lax.fori_loop(0, 7, functools.partial(block, steps=near), 0)
+        block(7, 0, near[:-1])
 
     pairs = ((signal_far, signal), (time_far.at[0], time.at[0]), (time_far.at[1], time.at[1]),
              (cut_far, cut), (wide_far, wide_all), (twist_far, twist), (upper_far, upper))

time: 34.9 us -> 33.9 us (0.971)
  Pallas kernels: 34.8 us -> 33.8 us
    pallas_call x1, Pallas kernels: 32.9 us -> 32 us  [body(): pl.pallas_call(functools.partial(filter_kernel, groups, inner), out_shape...]
where the time goes in v5:
time: 33.9 us; the launch traced here: 33.8 us
  Pallas kernels  33.8 us (100%)
    pallas_call x1, Pallas kernels, body(): pl.pallas_call(functools.partial(filter_kernel, groups, inner), out_shape...  32 us
    pallas_call x1, Pallas kernels, body(): pl.pallas_call(write_kernel, out_shape=jax.ShapeDtypeStruct((OWN, BAND *...  1.8 us

profile of v5, /device:TPU:1, one launch (start us, length us, event | category | flops | bytes accessed | tf_op | source)
XLA Modules:
  0.0 33.8 jit_solution(8380896718125674835)
XLA Ops:
  0.0 32.0 %fan_filter_products.1.lagged = f32[6144,128]{1,0:T(8,128)S(1)} custom-call(f32[128,1024]{1,0:T(8,128)} %signal_far.1, s32[128,128]{1,0:T(8,128)} %bitcast.1, bf16[2,512,1024]{2,1,0:T(8,128)(2,1)} %constant.8.clone.time_far, bf16[4,256,256]{2,1,0:T(8,128)(2,1)} %constant.9.clone.wide_far, f32[2,128,128]{2,1,0:T(8,128)} %constant.10.clone.twist_far, ...), custom_call_target="tpu_custom_call" | custom-call | tf_op jit(solution)/shard_map/fan_filter_products/pallas_call | solution.py:293
  32.0 1.8 %correlation_rows.1 = f32[128,4096]{1,0:T(8,128)} custom-call(f32[6144,128]{1,0:T(8,128)S(1)} %fan_filter_products.1.lagged), custom_call_target="tpu_custom_call" | custom-call | tf_op jit(solution)/shard_map/correlation_rows/pallas_call | solution.py:315

commit v6 on v5

--- a/solution.py
+++ b/solution.py
@@ -1,4 +1,5 @@
 import functools
+import itertools
 import math
 
 import jax
@@ -81,12 +82,17 @@
 def finish(lagged, out, first, last):
     lane = lax.broadcasted_iota(jnp.int32, (8, OWN), 1)
     odd = [(lane // step) % 2 == 1 for step in (1, 2, 4)]
+    known = {}
+
+    def skewed(bit, spot):
+        if (bit, spot) not in known:
+            known[bit, spot] = lagged[pl.ds(8 * spot, 8), :] if bit == 0 else jnp.where(
+                odd[bit - 1], skewed(bit - 1, spot + (1 << bit)), skewed(bit - 1, spot)
+            )
+        return known[bit, spot]
+
     for tile in range(first, last):
-        rows = [lagged[pl.ds(tile * OWN + 8 * number, 8), :] for number in range(TILE_ROWS + 14)]
-        for bit in range(3):
-            gap = 2 << bit
-            rows = [jnp.where(odd[bit], rows[spot + gap], rows[spot]) for spot in range(len(rows) - gap)]
-        turned = jnp.concatenate(rows, axis=0).T
+        turned = jnp.concatenate([skewed(3, tile * TILE_ROWS + number) for number in range(TILE_ROWS)], axis=0).T
         for group in range(max(0, tile - TILES + 1), min(TILE_ROWS, tile + 1)):
             out[pl.ds(8 * group, 8), pl.ds((tile - group) * OWN, OWN)] = turned[8 * group:8 * group + 8]
 
@@ -115,20 +121,15 @@
         highs, cores, tops = (8 * high, 8 - 8 * high), (core, 1 - core), (4 * top, 4 - 4 * top)
         mids = [2 * lax.rem(mid + step, 4) for step in range(4)]
         lows = [lax.rem(low + step, 4) for step in range(4)]
-        far = ((2, 2), (1, 3), (3, 1), (1, 1), (3, 3), (2, 1), (1, 2), (2, 3), (3, 2))
-        near = ((2, 0), (0, 2), (1, 0), (0, 3), (3, 0), (0, 1), (0, 0))
-
-        def block(index, carry, steps):
-            cx = jnp.where(lax.rem(index // 2, 2) == 0, highs[1], highs[0])
-            cx = cx + jnp.where(lax.rem(index, 2) == 0, cores[1], cores[0])
-            cy = jnp.where(index // 4 == 0, tops[1], tops[0])
-            for mid_step, low_step in steps:
-                visit(cx + mids[mid_step], cy + lows[low_step])
-            return carry
-
-        lax.fori_loop(0, 8, functools.partial(block, steps=far), 0)
-        lax.fori_loop(0, 7, functools.partial(block, steps=near), 0)
-        block(7, 0, near[:-1])
+        ring = (0, 1, 2, 1)
+        offsets = sorted(
+            itertools.product(range(4), range(4), range(2), range(2), range(2)),
+            key=lambda o: (-(ring[o[0]] + ring[o[1]] + 2 * o[2] + o[3]),
+                           (o[0] * 7 + o[1] * 5 + o[2] * 3 + o[3] * 11 + o[4] * 13) % 17),
+        )
+        for mid_step, low_step, flip_top, flip_high, flip_core in offsets:
+            if mid_step + low_step + flip_top + flip_high + flip_core > 0:
+                visit(highs[flip_high] + mids[mid_step] + cores[flip_core], tops[flip_top] + lows[low_step])
 
     pairs = ((signal_far, signal), (time_far.at[0], time.at[0]), (time_far.at[1], time.at[1]),
              (cut_far, cut), (wide_far, wide_all), (twist_far, twist), (upper_far, upper))

time: 33.9 us -> 33.5 us (0.988)
  Pallas kernels: 33.8 us -> 33.4 us
    pallas_call x1, Pallas kernels: 32 us -> 31.6 us  [body(): pl.pallas_call(functools.partial(filter_kernel, groups, inner), out_shape...]
where the time goes in v6:
time: 33.5 us; the launch traced here: 33.4 us
  Pallas kernels  33.4 us (100%)
    pallas_call x1, Pallas kernels, body(): pl.pallas_call(functools.partial(filter_kernel, groups, inner), out_shape...  31.6 us
    pallas_call x1, Pallas kernels, body(): pl.pallas_call(write_kernel, out_shape=jax.ShapeDtypeStruct((OWN, BAND *...  1.8 us

profile of v6, /device:TPU:1, one launch (start us, length us, event | category | flops | bytes accessed | tf_op | source)
XLA Modules:
  0.0 33.4 jit_solution(12849392414472630519)
XLA Ops:
  0.0 31.6 %fan_filter_products.1.lagged = f32[6144,128]{1,0:T(8,128)S(1)} custom-call(f32[128,1024]{1,0:T(8,128)} %signal_far.1, s32[128,128]{1,0:T(8,128)} %bitcast.1, bf16[2,512,1024]{2,1,0:T(8,128)(2,1)} %constant.8.clone.time_far, bf16[4,256,256]{2,1,0:T(8,128)(2,1)} %constant.9.clone.wide_far, f32[2,128,128]{2,1,0:T(8,128)} %constant.10.clone.twist_far, ...), custom_call_target="tpu_custom_call" | custom-call | tf_op jit(solution)/shard_map/fan_filter_products/pallas_call | solution.py:294
  31.6 1.8 %correlation_rows.1 = f32[128,4096]{1,0:T(8,128)} custom-call(f32[6144,128]{1,0:T(8,128)S(1)} %fan_filter_products.1.lagged), custom_call_target="tpu_custom_call" | custom-call | tf_op jit(solution)/shard_map/correlation_rows/pallas_call | solution.py:316

commit v7 on v6

--- a/solution.py
+++ b/solution.py
@@ -55,14 +55,6 @@
     return dot(left[0], right[0]) + (dot(left[0], right[1]) + dot(left[1], right[0]))
 
 
-def blocks(value):
-    return value[:OWN, :OWN], value[:OWN, OWN:], value[OWN:, :OWN], value[OWN:, OWN:]
-
-
-def join(a, b, c, d):
-    return jnp.concatenate([jnp.concatenate([a, b], axis=1), jnp.concatenate([c, d], axis=1)], axis=0)
-
-
 def least_cut(cut):
     row = lax.broadcasted_iota(jnp.int32, (OWN, OWN), 0)
     col = lax.broadcasted_iota(jnp.int32, (OWN, OWN), 1)
@@ -206,26 +198,29 @@
     settle(out_first, in_first, send_first, recv_first)
 
     rows = [in_first[:, part, :] for part in range(4)]
-    value = dot_three(wide, split(join(rows[0], rows[1], rows[2] * jnp.where(me == 0, 0.0, 1.0), rows[3])))
-    re_a, re_b, im_a, im_b = blocks(value)
-    value = join(
-        re_a * cosine + im_a * sine, im_a * cosine - re_a * sine,
-        re_b * cosine + im_b * sine, im_b * cosine - re_b * sine,
-    )
-    value = dot_three(split(value), flip)
+    real_zero = rows[2] * jnp.where(me == 0, 0.0, 1.0)
+    values = [jnp.concatenate(pair, axis=0) for pair in ((rows[0], real_zero), (rows[1], rows[3]))]
+    values = [dot_three(wide, split(value)) for value in values]
+    values = [
+        jnp.concatenate([re * cosine + im * sine, im * cosine - re * sine], axis=1)
+        for re, im in ((value[:OWN], value[OWN:]) for value in values)
+    ]
+    values = [dot_three(split(value), flip) for value in values]
     even = (2 * me).astype(F32)
     scale = -2.0 / (LENGTH * groups * OWN)
-    keep_a = jnp.where(cut_least > even, jnp.where(me == 0, 0.5 * scale, scale), 0.0)
-    keep_b = jnp.where(cut_least > even + 1.0, scale, 0.0)
-    value = value * join(keep_a, keep_a, keep_b, keep_b)
-    value = dot_three(split(value), wide)
-    re_a, im_a, re_b, im_b = blocks(value)
-    value = join(
-        re_a * cosine - im_a * sine, re_b * cosine - im_b * sine,
-        im_a * cosine + re_a * sine, im_b * cosine + re_b * sine,
+    rejects = (
+        jnp.where(cut_least > even, jnp.where(me == 0, 0.5 * scale, scale), 0.0),
+        jnp.where(cut_least > even + 1.0, scale, 0.0),
     )
-    value = dot_three(flip, split(value))
-    for part, block in enumerate(blocks(value)):
+    values = [value * jnp.concatenate([reject, reject], axis=1) for value, reject in zip(values, rejects)]
+    values = [dot_three(split(value), wide) for value in values]
+    values = [
+        jnp.concatenate([re * cosine - im * sine, im * cosine + re * sine], axis=0)
+        for re, im in ((value[:, :OWN], value[:, OWN:]) for value in values)
+    ]
+    values = [dot_three(flip, split(value)) for value in values]
+    for part in range(4):
+        block = values[part % 2][(part // 2) * OWN:(part // 2 + 1) * OWN]
         weight = 2.0 / LENGTH if part % 2 else jnp.where(me == 0, 1.0 / LENGTH, 2.0 / LENGTH)
         kept = rows[part] * weight + block
         for first, array in (
@@ -293,7 +288,7 @@
     messages = [pltpu.VMEM((groups, 4, OWN), F32)] * 2 + [pltpu.VMEM((groups, PACK, OWN), BF16)] * 2
     lagged = pl.pallas_call(
         functools.partial(filter_kernel, groups, inner),
-        out_shape=pltpu.VMEM((3 * OWN * LAGS, OWN), F32),
+        out_shape=pltpu.VMEM(((3 * OWN + 1) * LAGS, OWN), F32),
         in_specs=[far] * len(operands),
         out_specs=pl.BlockSpec(memory_space=pltpu.VMEM),
         scratch_shapes=[pltpu.VMEM(array.shape, array.dtype) for array in operands]
@@ -303,7 +298,7 @@
             pltpu.VMEM((OWN, 2 * BINS), BF16),
             pltpu.VMEM((2, OWN, 2 * BINS), BF16),
             pltpu.VMEM((2 * OWN, LENGTH), F32),
-            pltpu.VMEM((PACK * (groups + 2), OWN), F32),
+            pltpu.VMEM((PACK * (groups + 4), OWN), F32),
             pltpu.VMEM((3 * OWN, LENGTH), BF16),
             pltpu.VMEM((LAGS * OWN, LENGTH), BF16),
         ],

time: 33.5 us -> 33.2 us (level)
  no operation moved by 1% of the time
where the time goes in v7:
time: 33.2 us; the launch traced here: 33.1 us
  Pallas kernels  33.1 us (100%)
    pallas_call x1, Pallas kernels, body(): pl.pallas_call(functools.partial(filter_kernel, groups, inner), out_shape...  31.3 us
    pallas_call x1, Pallas kernels, body(): pl.pallas_call(write_kernel, out_shape=jax.ShapeDtypeStruct((OWN, BAND *...  1.8 us

profile of v7, /device:TPU:1, one launch (start us, length us, event | category | flops | bytes accessed | tf_op | source)
XLA Modules:
  0.0 33.1 jit_solution(9926396898765360709)
XLA Ops:
  0.0 31.3 %fan_filter_products.1.lagged = f32[6160,128]{1,0:T(8,128)S(1)} custom-call(f32[128,1024]{1,0:T(8,128)} %signal_far.1, s32[128,128]{1,0:T(8,128)} %bitcast.1, bf16[2,512,1024]{2,1,0:T(8,128)(2,1)} %constant.8.clone.time_far, bf16[4,256,256]{2,1,0:T(8,128)(2,1)} %constant.9.clone.wide_far, f32[2,128,128]{2,1,0:T(8,128)} %constant.10.clone.twist_far, ...), custom_call_target="tpu_custom_call" | custom-call | tf_op jit(solution)/shard_map/fan_filter_products/pallas_call | solution.py:289
  31.3 1.8 %correlation_rows.1 = f32[128,4096]{1,0:T(8,128)} custom-call(f32[6160,128]{1,0:T(8,128)S(1)} %fan_filter_products.1.lagged), custom_call_target="tpu_custom_call" | custom-call | tf_op jit(solution)/shard_map/correlation_rows/pallas_call | solution.py:311

commit v8 on v7

--- a/solution.py
+++ b/solution.py
@@ -74,6 +74,7 @@
 def finish(lagged, out, first, last):
     lane = lax.broadcasted_iota(jnp.int32, (8, OWN), 1)
     odd = [(lane // step) % 2 == 1 for step in (1, 2, 4)]
+    odd_lag = lax.broadcasted_iota(jnp.int32, (OWN, OWN), 1) % 2 == 1
     known = {}
 
     def skewed(bit, spot):
@@ -85,6 +86,8 @@
 
     for tile in range(first, last):
         turned = jnp.concatenate([skewed(3, tile * TILE_ROWS + number) for number in range(TILE_ROWS)], axis=0).T
+        swapped = jnp.concatenate([turned[OWN // 2:], turned[:OWN // 2]], axis=0)
+        turned = jnp.where(odd_lag, swapped, turned)
         for group in range(max(0, tile - TILES + 1), min(TILE_ROWS, tile + 1)):
             out[pl.ds(8 * group, 8), pl.ds((tile - group) * OWN, OWN)] = turned[8 * group:8 * group + 8]
 
@@ -257,16 +260,28 @@
         ext[pl.ds(0, OWN), span] = (upper_sides[pl.ds(0, OWN), span] + sums[2 * OWN:3 * OWN]).astype(BF16)
         ext[pl.ds(2 * OWN, OWN), span] = (upper_sides[pl.ds(OWN, OWN), span] + sums[3 * OWN:]).astype(BF16)
     own = ext[pl.ds(OWN, OWN), :] * jnp.asarray(1.0 / math.sqrt(LENGTH), BF16)
+    half = OWN // 2
     for lag in range(LAGS):
-        lags[pl.ds(lag * OWN, OWN), :] = own if lag == 0 else jnp.concatenate(
+        shifted = own if lag == 0 else jnp.concatenate(
             [jnp.zeros((OWN, lag), BF16), own[:, :LENGTH - lag]], axis=1
         )
-
-    everything = ext[...]
-    for number in range(LAGS // 2):
-        values = dot(everything, lags[pl.ds(number * 2 * OWN, 2 * OWN), :], ((1,), (1,)))
-        for side in range(2):
-            lagged[pl.ds(2 * number + side, 3 * OWN, stride=LAGS), :] = values[:, side * OWN:(side + 1) * OWN]
+        lags[0, pl.ds(lag * half, half), :] = shifted[:half]
+        lags[1, pl.ds((lag ^ 1) * half, half), :] = shifted[half:]
+
+    span = 3 * OWN - half
+    front = lax.broadcasted_iota(jnp.int32, (span - half, OWN), 1) < half
+    for number in range(LAGS // 4):
+        rows = pl.ds(number * 4 * half, 4 * half)
+        first = dot(ext[pl.ds(0, span), :], lags[0, rows, :], ((1,), (1,)))
+        second = dot(ext[pl.ds(half, span), :], lags[1, rows, :], ((1,), (1,)))
+        for lag in range(4):
+            lanes = slice(lag // 2 * OWN, (lag // 2 + 1) * OWN)
+            begin = 4 * number + lag
+            low, high = first[:, lanes], second[:, lanes]
+            both = (low[half:], high[:span - half])
+            lagged[pl.ds(begin, half, stride=LAGS), :] = low[:half]
+            lagged[pl.ds(half * LAGS + begin, span - half, stride=LAGS), :] = jnp.where(front, both[lag % 2], both[1 - lag % 2])
+            lagged[pl.ds(span * LAGS + begin, half, stride=LAGS), :] = high[span - half:]
     for copy in early:
         copy.wait_send()
 
@@ -300,7 +315,7 @@
             pltpu.VMEM((2 * OWN, LENGTH), F32),
             pltpu.VMEM((PACK * (groups + 4), OWN), F32),
             pltpu.VMEM((3 * OWN, LENGTH), BF16),
-            pltpu.VMEM((LAGS * OWN, LENGTH), BF16),
+            pltpu.VMEM((2, LAGS * OWN // 2, LENGTH), BF16),
         ],
         compiler_params=pltpu.CompilerParams(
             collective_id=0, has_side_effects=True, vmem_limit_bytes=40 * 2**20

time: 33.2 us -> 33 us (level)
  no operation moved by 1% of the time
where the time goes in v8:
time: 33 us; the launch traced here: 32.9 us
  Pallas kernels  32.9 us (100%)
    pallas_call x1, Pallas kernels, body(): pl.pallas_call(functools.partial(filter_kernel, groups, inner), out_shape...  31.1 us
    pallas_call x1, Pallas kernels, body(): pl.pallas_call(write_kernel, out_shape=jax.ShapeDtypeStruct((OWN, BAND *...  1.8 us

profile of v8, /device:TPU:1, one launch (start us, length us, event | category | flops | bytes accessed | tf_op | source)
XLA Modules:
  0.0 32.9 jit_solution(13212156498663944489)
XLA Ops:
  0.0 31.1 %fan_filter_products.1.lagged = f32[6160,128]{1,0:T(8,128)S(1)} custom-call(f32[128,1024]{1,0:T(8,128)} %signal_far.1, s32[128,128]{1,0:T(8,128)} %bitcast.1, bf16[2,512,1024]{2,1,0:T(8,128)(2,1)} %constant.8.clone.time_far, bf16[4,256,256]{2,1,0:T(8,128)(2,1)} %constant.9.clone.wide_far, f32[2,128,128]{2,1,0:T(8,128)} %constant.10.clone.twist_far, ...), custom_call_target="tpu_custom_call" | custom-call | tf_op jit(solution)/shard_map/fan_filter_products/pallas_call | solution.py:304
  31.1 1.8 %correlation_rows.1 = f32[128,4096]{1,0:T(8,128)} custom-call(f32[6160,128]{1,0:T(8,128)S(1)} %fan_filter_products.1.lagged), custom_call_target="tpu_custom_call" | custom-call | tf_op jit(solution)/shard_map/correlation_rows/pallas_call | solution.py:326

commit v9 on v7

--- a/solution.py
+++ b/solution.py
@@ -172,7 +172,8 @@
             device_id=at(peer(1)),
             device_id_type=MESH,
         )
-        rest.wait()
+        rest.wait_recv()
+        return rest
 
     exchange(out_first, in_first, send_first, recv_first)
     for load in loads[3:]:
@@ -195,7 +196,7 @@
     wide = (wide_all[0], wide_all[1])
     flip = (wide_all[2], wide_all[3])
     cosine, sine = twist[0], twist[1]
-    settle(out_first, in_first, send_first, recv_first)
+    sent_first = settle(out_first, in_first, send_first, recv_first)
 
     rows = [in_first[:, part, :] for part in range(4)]
     real_zero = rows[2] * jnp.where(me == 0, 0.0, 1.0)
@@ -238,7 +239,7 @@
     row = lax.broadcasted_iota(jnp.int32, (2 * OWN, LENGTH), 0)
     inside = jnp.where(row < OWN, (me > 0).astype(F32), (me < groups - 1).astype(F32))
     upper_sides[...] = (dot(bins, upper[0]) + dot(bins, upper[1])) * inside
-    settle(out_second, in_second, send_second, recv_second)
+    sent_second = settle(out_second, in_second, send_second, recv_second)
 
     packed[pl.ds(0, PACK * groups), :] = in_second[...].astype(F32).reshape(PACK * groups, OWN)
 
@@ -267,7 +268,7 @@
         values = dot(everything, lags[pl.ds(number * 2 * OWN, 2 * OWN), :], ((1,), (1,)))
         for side in range(2):
             lagged[pl.ds(2 * number + side, 3 * OWN, stride=LAGS), :] = values[:, side * OWN:(side + 1) * OWN]
-    for copy in early:
+    for copy in (sent_first, sent_second, *early):
         copy.wait_send()
 
 

time: 33.2 us -> 33.2 us (level)
  no operation moved by 1% of the time
where the time goes in v9:
time: 33.2 us; the launch traced here: 33.1 us
  Pallas kernels  33.1 us (100%)
    pallas_call x1, Pallas kernels, body(): pl.pallas_call(functools.partial(filter_kernel, groups, inner), out_shape...  31.3 us
    pallas_call x1, Pallas kernels, body(): pl.pallas_call(write_kernel, out_shape=jax.ShapeDtypeStruct((OWN, BAND *...  1.8 us

profile of v9, /device:TPU:1, one launch (start us, length us, event | category | flops | bytes accessed | tf_op | source)
XLA Modules:
  0.0 33.1 jit_solution(5273139366905787018)
XLA Ops:
  0.0 31.3 %fan_filter_products.1.lagged = f32[6160,128]{1,0:T(8,128)S(1)} custom-call(f32[128,1024]{1,0:T(8,128)} %signal_far.1, s32[128,128]{1,0:T(8,128)} %bitcast.1, bf16[2,512,1024]{2,1,0:T(8,128)(2,1)} %constant.8.clone.time_far, bf16[4,256,256]{2,1,0:T(8,128)(2,1)} %constant.9.clone.wide_far, f32[2,128,128]{2,1,0:T(8,128)} %constant.10.clone.twist_far, ...), custom_call_target="tpu_custom_call" | custom-call | tf_op jit(solution)/shard_map/fan_filter_products/pallas_call | solution.py:290
  31.3 1.8 %correlation_rows.1 = f32[128,4096]{1,0:T(8,128)} custom-call(f32[6160,128]{1,0:T(8,128)S(1)} %fan_filter_products.1.lagged), custom_call_target="tpu_custom_call" | custom-call | tf_op jit(solution)/shard_map/correlation_rows/pallas_call | solution.py:312
